TPU v7x, 512 devices: a whole 4x4x16 slice. The times are simulated.
512 devices in a mesh: ctx: 32 (over z, x_hi), head: 16 (over y, x_lo, core).
Axes of the slice: x: 4 (x_hi: 2, x_lo: 2; x = x_hi * 2 + x_lo), y: 4, z: 16, core: 2. Of those that a mesh axis runs over, the one named last changes fastest.
Arguments:
- queries: bfloat16 [4096, 4096], P('ctx', 'head'), may hold values from -5 to 5
- keys: bfloat16 [4096, 4096], P('ctx', 'head'), may hold values from -5 to 5
- values: bfloat16 [4096, 4096], P('ctx', 'head'), may hold values from -6 to 6
- episode: int32 [4096], P('ctx'), may hold values from 0 to 126, as said below
- out_weight: bfloat16 [4096, 4096], P('head'), may hold values from -1.5 to 1.5
- d_out: bfloat16 [4096, 4096], P(('ctx', 'head')), may hold values from -0.3984375 to 0.3984375
Outputs:
- mixed: bfloat16 [4096, 4096], P(('ctx', 'head'))
- d_queries: bfloat16 [4096, 4096], P('ctx', 'head')
- d_keys: bfloat16 [4096, 4096], P('ctx', 'head')
- d_values: bfloat16 [4096, 4096], P('ctx', 'head')
Inputs may be any that keep to these rules, and one draw needn't show every extreme that they name: Episode numbers never fall as time rises; the episode of time step t is 0 for t < 64 and 2 * (t // 64) - 1 or 2 * (t // 64) otherwise (so each episode has 1 to 64 time steps, and episode 0 has exactly 64).
All inputs are finite; a program needn't handle non-finite values.
Results may differ from a plain program's by a relative error of at most 0.02.
Values may be sent and summed in bfloat16 or wider, within the bound.
No kernel may reach another device: no remote copies, remote signals or barrier semaphores. Data moves between devices by JAX's collectives and lax.ppermute only.
A program may use at most 64 MiB of HBM per device.

v0:
```python
import jax
import jax.numpy as jnp
from jax import lax
from jax.sharding import PartitionSpec as P

HD = 128


floor_score = -1e30


def time_steps(rows, rows_local, ctx_count):
    half_rows = rows_local // 2
    holder = rows // rows_local
    offset = rows % rows_local
    return jnp.where(
        offset < half_rows,
        holder * half_rows + offset,
        (2 * ctx_count - 1 - holder) * half_rows + offset - half_rows,
    )


def on_device(queries, keys, values, episode, out_weight, d_out):
    rows_local = queries.shape[0]
    width = queries.shape[1]
    heads = width // HD
    scale = HD ** (-0.5)
    place = lax.axis_index("ctx")
    ctx_count = lax.axis_size("ctx")
    window = 2 * ctx_count
    d_attn = lax.dot_general(
        lax.all_gather(d_out, "head", axis=0, tiled=True),
        out_weight,
        (((1,), (1,)), ((), ())),
        preferred_element_type=jnp.float32,
    ).astype(jnp.bfloat16)
    keys_all, values_all, episode_all = (
        lax.all_gather(keys, "ctx", axis=0, tiled=True),
        lax.all_gather(values, "ctx", axis=0, tiled=True),
        lax.all_gather(episode, "ctx", axis=0, tiled=True),
    )
    total = keys_all.shape[0]
    query_pos = place * rows_local + jnp.arange(rows_local, dtype=jnp.int32)
    query_time = time_steps(query_pos, rows_local, ctx_count)
    key_time = time_steps(jnp.arange(total, dtype=jnp.int32), rows_local, ctx_count)
    visible = (key_time[None, :] <= query_time[:, None]) & (
        episode[:, None] - episode_all[None, :] < window
    )
    query_heads = queries.reshape(rows_local, heads, HD)
    key_heads = keys_all.reshape(total, heads, HD)
    value_heads = values_all.reshape(total, heads, HD)
    scores = (
        jnp.einsum("qhd,khd->hqk", query_heads, key_heads, preferred_element_type=jnp.float32)
        * scale
    )
    scores = jnp.where(visible[None], scores, floor_score)
    top = jnp.max(scores, axis=2)
    lse = top + jnp.log(jnp.sum(jnp.exp(scores - top[:, :, None]), axis=2))
    probs = jnp.exp(scores - lse[:, :, None])
    probs_low = probs.astype(jnp.bfloat16)
    attn_heads = jnp.einsum(
        "hqk,khd->qhd", probs_low, value_heads, preferred_element_type=jnp.float32
    ).astype(jnp.bfloat16)
    attn = attn_heads.reshape(rows_local, width)
    mixed = lax.psum_scatter(
        jnp.dot(attn, out_weight, preferred_element_type=jnp.float32),
        "head",
        scatter_dimension=0,
        tiled=True,
    ).astype(jnp.bfloat16)
    d_heads = d_attn.reshape(rows_local, heads, HD)
    delta = jnp.sum(d_heads.astype(jnp.float32) * attn_heads.astype(jnp.float32), axis=2).T
    d_probs = jnp.einsum("qhd,khd->hqk", d_heads, value_heads, preferred_element_type=jnp.float32)
    d_scores = (probs * (d_probs - delta[:, :, None])).astype(jnp.bfloat16)
    dq_sum = jnp.einsum("hqk,khd->qhd", d_scores, key_heads, preferred_element_type=jnp.float32)
    d_queries = (scale * dq_sum).astype(jnp.bfloat16).reshape(rows_local, width)
    lse_all, delta_all = (
        lax.all_gather(lse.T, "ctx", axis=0, tiled=True),
        lax.all_gather(delta.T, "ctx", axis=0, tiled=True),
    )
    own_keys = keys.reshape(rows_local, heads, HD)
    own_values = values.reshape(rows_local, heads, HD)
    piece_q = lax.all_gather(queries, "ctx", axis=0, tiled=True)
    piece_d = lax.all_gather(d_attn, "ctx", axis=0, tiled=True)
    piece_ep = lax.all_gather(episode, "ctx", axis=0, tiled=True)
    count = piece_q.shape[0]
    piece_qh = piece_q.reshape(count, heads, HD)
    piece_dh = piece_d.reshape(count, heads, HD)
    piece_pos = jnp.arange(count, dtype=jnp.int32)
    piece_time = time_steps(piece_pos, rows_local, ctx_count)
    piece_mask = (query_time[None, :] <= piece_time[:, None]) & (
        piece_ep[:, None] - episode[None, :] < window
    )
    piece_scores = (
        jnp.einsum("qhd,khd->hqk", piece_qh, own_keys, preferred_element_type=jnp.float32) * scale
    )
    piece_scores = jnp.where(piece_mask[None], piece_scores, floor_score)
    piece_lse = lse_all.T
    piece_delta = delta_all.T
    piece_probs = jnp.exp(piece_scores - piece_lse[:, :, None])
    piece_dprobs = jnp.einsum(
        "qhd,khd->hqk", piece_dh, own_values, preferred_element_type=jnp.float32
    )
    piece_ds = (piece_probs * (piece_dprobs - piece_delta[:, :, None])).astype(jnp.bfloat16)
    dk_sum = jnp.einsum("hqk,qhd->khd", piece_ds, piece_qh, preferred_element_type=jnp.float32)
    dv_sum = jnp.einsum(
        "hqk,qhd->khd",
        piece_probs.astype(jnp.bfloat16),
        piece_dh,
        preferred_element_type=jnp.float32,
    )
    d_keys = (scale * dk_sum).astype(jnp.bfloat16).reshape(rows_local, width)
    d_values = dv_sum.astype(jnp.bfloat16).reshape(rows_local, width)
    return (mixed, d_queries, d_keys, d_values)


def solution(mesh):
    placed = (
        P("ctx", "head"),
        P("ctx", "head"),
        P("ctx", "head"),
        P("ctx"),
        P("head", None),
        P(("ctx", "head"), None),
    )
    return jax.shard_map(
        on_device,
        mesh=mesh,
        in_specs=placed,
        out_specs=(P(("ctx", "head"), None), P("ctx", "head"), P("ctx", "head"), P("ctx", "head")),
        check_vma=False,
    )
```

profile of v0, /device:TPU:4, one launch (start us, length us, event | category | flops | bytes accessed | tf_op | source)
XLA Modules:
  0.0 720.3 jit_solution(6676327848458091657)
XLA Ops:
  7.2 0.0 copy-start
  7.2 0.0 copy-start.6
  7.2 0.0 all-gather.11.cloned.1.call-start
  7.2 0.7 all-gather.11.cloned.1.call-update
  7.9 0.0 all-gather.9.cloned.1.call-start
  8.0 0.7 all-gather.9.cloned.1.call-update
  8.7 0.0 all-gather.7.cloned.1.call-start
  8.7 1.6 copy.32
  10.3 0.0 all-gather.7.cloned.1.call-update
  10.3 0.0 all-gather.13.cloned.1.call-start
  10.4 1.6 copy.39
  11.9 0.0 all-gather.13.cloned.1.call-update
  12.0 0.0 all-gather.15.cloned.1.call-start
  12.0 42.5 %all-gather.11.cloned.1.call-done = bf16[128,4096]{1,0:T(8,128)(2,1)} async-done(((bf16[8,4096]{1,0:T(8,128)(2,1)}), bf16[128,4096]{1,0:T(8,128)(2,1)}) %all-gather.11.cloned.1.call-update) | async-done | bytes 1048592 | tf_op jit(solution)/shard_map/all_gather | solution.py:32
  54.5 0.0 copy-done
  54.5 2.7 convolution_convert_fusion
  57.2 0.0 all-gather.15.cloned.1.call-update
  57.2 0.0 reduce-scatter.2.cloned.1.call-start
  57.3 0.0 copy-done.6
  57.3 72.2 %all-gather = s32[32,1,128]{2,1,0:T(1,128)S(1)} all-gather(s32[1,1,128]{2,1,0:T(1,128)S(1)} %bitcast.82), channel_id=1, replica_groups=mesh['ctx'=32,'head'=16] {'ctx'}, dimensions={0}, use_global_device_ids=true | all-gather | bytes 16896 | tf_op jit(solution)/shard_map/all_gather | solution.py:40
  129.5 0.5 fusion.14
  130.0 1.0 copy.36
  131.0 0.0 copy-start.3
  131.0 74.7 %all-gather.9.cloned.1.call-done = bf16[4096,256]{1,0:T(8,128)(2,1)} async-done(((bf16[128,256]{1,0:T(8,128)(2,1)}), bf16[4096,256]{1,0:T(8,128)(2,1)}) %all-gather.9.cloned.1.call-update) | async-done | bytes 2097168 | tf_op jit(solution)/shard_map/all_gather | solution.py:39
  205.7 4.1 copy.35
  209.8 139.5 %all-gather.7.cloned.1.call-done = bf16[4096,256]{0,1:T(8,128)(2,1)} async-done(((bf16[128,256]{0,1:T(8,128)(2,1)}), bf16[4096,256]{0,1:T(8,128)(2,1)}) %all-gather.7.cloned.1.call-update) | async-done | bytes 2097168 | tf_op jit(solution)/shard_map/all_gather | solution.py:38
  349.3 0.0 copy-done.3
  349.3 2.8 fusion.51
  352.1 0.0 copy-start.1
  352.1 0.0 copy-start.2
  352.1 0.7 exponential_reduce_fusion
  352.8 1.4 copy-done.1
  354.2 1.0 copy-done.2
  355.2 0.8 multiply_reduce_fusion
  356.0 1.8 fusion.52
  357.8 0.0 reduce-scatter.2.cloned.1.call-update
  357.9 1.4 fusion.15
  359.3 0.0 copy-start.5
  359.3 5.2 fusion.20
  364.5 0.7 copy.45
  365.2 73.4 %all_gather.32 = f32[4096,2]{0,1:T(2,128)S(1)} all-gather(f32[128,2]{0,1:T(2,128)S(1)} %get-tuple-element.18), channel_id=1, replica_groups=mesh['ctx'=32,'head'=16] {'ctx'}, dimensions={0}, use_global_device_ids=true | all-gather | bytes 33792 | tf_op jit(solution)/shard_map/all_gather | solution.py:79
  438.7 73.0 %all_gather.30 = f32[4096,2]{0,1:T(2,128)S(1)} all-gather(f32[128,2]{0,1:T(2,128)S(1)} %bitcast.80), channel_id=1, replica_groups=mesh['ctx'=32,'head'=16] {'ctx'}, dimensions={0}, use_global_device_ids=true | all-gather | bytes 33792 | tf_op jit(solution)/shard_map/all_gather | solution.py:78
  511.6 0.0 all-gather.13.cloned.1.call-done
  511.6 0.0 copy-done.5
  511.6 4.5 fusion.3
  516.2 0.0 copy-start.4
  516.2 124.4 %all-gather.15.cloned.1.call-done = bf16[4096,256]{1,0:T(8,128)(2,1)} async-done(((bf16[128,256]{1,0:T(8,128)(2,1)}), bf16[4096,256]{1,0:T(8,128)(2,1)}) %all-gather.15.cloned.1.call-update) | async-done | bytes 2097168 | tf_op jit(solution)/shard_map/all_gather | solution.py:84
  640.5 4.1 copy.52
  644.6 0.0 copy-done.4
  644.6 5.4 fusion.21
  650.1 0.7 copy.46
  650.8 3.5 fusion.22
  654.3 0.7 copy.47
  655.1 56.8 %reduce-scatter.2.cloned.1.call-done = f32[8,4096]{1,0:T(8,128)} async-done(((f32[128,4096]{1,0:T(8,128)}), f32[8,4096]{1,0:T(8,128)}) %reduce-scatter.2.cloned.1.call-update) | async-done | bytes 131088 | tf_op jit(solution)/shard_map/reduce_scatter | solution.py:65
  711.9 1.5 convert_element_type.51
  (3 shorter events, 0.0 us)
Async XLA Ops:
  7.2 47.3 %copy-start = (bf16[256,4096]{1,0:T(8,128)(2,1)S(1)}, bf16[256,4096]{1,0:T(8,128)(2,1)}, u32[]{:S(2)}) copy-start(bf16[256,4096]{1,0:T(8,128)(2,1)} %param.10) | copy-start | bytes 6291460
  7.2 50.1 %copy-start.6 = (s32[128]{0:T(128)S(1)}, s32[128]{0:T(128)}, u32[]{:S(2)}) copy-start(s32[128]{0:T(128)} %param.9) | copy-start | bytes 1540
  7.2 47.3 %all-gather.11.cloned.1.call-start = ((), (), s32[]{:S(2)}) async-start(), calls=%async_computation.4 | async-start | bytes 1114112 | tf_op jit(solution)/shard_map/all_gather | solution.py:32
  7.9 197.8 %all-gather.9.cloned.1.call-start = ((), (), s32[]{:S(2)}) async-start(), calls=%async_computation.2 | async-start | bytes 2162688 | tf_op jit(solution)/shard_map/all_gather | solution.py:39
  8.7 340.6 %all-gather.7.cloned.1.call-start = ((), (), s32[]{:S(2)}) async-start(), calls=%async_computation.1 | async-start | bytes 2162688 | tf_op jit(solution)/shard_map/all_gather | solution.py:38
  10.3 501.3 %all-gather.13.cloned.1.call-start = ((), (), s32[]{:S(2)}) async-start(), calls=%async_computation.5 | async-start | bytes 2162688 | tf_op jit(solution)/shard_map/all_gather | solution.py:83
  12.0 628.6 %all-gather.15.cloned.1.call-start = ((), (), s32[]{:S(2)}) async-start(), calls=%async_computation.6 | async-start | bytes 2162688 | tf_op jit(solution)/shard_map/all_gather | solution.py:84
  57.2 654.7 %reduce-scatter.2.cloned.1.call-start = ((), (), s32[]{:S(2)}) async-start(), calls=%async_computation.3 | async-start | bytes 2228224 | tf_op jit(solution)/shard_map/reduce_scatter | solution.py:65
  131.0 218.3 %copy-start.3 = (bf16[128,256]{1,0:T(8,128)(2,1)S(1)}, bf16[128,256]{1,0:T(8,128)(2,1)}, u32[]{:S(2)}) copy-start(bf16[128,256]{1,0:T(8,128)(2,1)} %param.6) | copy-start | bytes 196612
  352.1 2.1 copy-start.1
  352.1 3.1 copy-start.2
  359.3 152.3 %copy-start.5 = (bf16[128,256]{1,0:T(8,128)(2,1)S(1)}, bf16[128,256]{1,0:T(8,128)(2,1)}, u32[]{:S(2)}) copy-start(bf16[128,256]{1,0:T(8,128)(2,1)} %param.7) | copy-start | bytes 196612
  516.2 128.5 %copy-start.4 = (bf16[128,256]{1,0:T(8,128)(2,1)S(1)}, bf16[128,256]{1,0:T(8,128)(2,1)}, u32[]{:S(2)}) copy-start(bf16[128,256]{1,0:T(8,128)(2,1)} %param.8) | copy-start | bytes 196612
Sparse Core Ops, SparseCore 0:
  10.2 44.2 all-gather.10
  57.6 148.0 all-gather.8
  209.2 140.0 all-gather.6
  352.6 140.4 all-gather.12
  496.6 143.9 all-gather.14
  643.2 68.6 reduce-scatter.1
where the time goes:
time: 721 us; the launch traced here: 720 us
  waiting for transfers between devices  439 us (61%)
  blocking collectives  219 us (30%)
  matrix products  26.8 us (4%)
  local copies, waits for them, and re-layouts  16.9 us (2%)
  between operations  14.2 us (2%)
    all_gather x1, waiting for transfers between devices, on_device(): lax.all_gather(keys, 'ctx', axis=0, tiled=True)  139 us
    all_gather x1, waiting for transfers between devices, on_device(): piece_d = lax.all_gather(d_attn, 'ctx', axis=0, tiled=True)  124 us
    all_gather x1, waiting for transfers between devices, on_device(): lax.all_gather(values, 'ctx', axis=0, tiled=True)  74.7 us
    all_gather x1, blocking collectives, on_device(): lax.all_gather(delta.T, 'ctx', axis=0, tiled=True)  73.4 us
    all_gather x1, blocking collectives, on_device(): lax.all_gather(lse.T, 'ctx', axis=0, tiled=True)  73 us
    all_gather x1, blocking collectives, on_device(): lax.all_gather(episode, 'ctx', axis=0, tiled=True)  72.2 us
    reduce_scatter x1, waiting for transfers between devices, on_device(): lax.psum_scatter(jnp.dot(attn, out_weight, preferred_element_type=jnp.flo...  56.8 us
    all_gather x1, waiting for transfers between devices, on_device(): lax.all_gather(d_out, 'head', axis=0, tiled=True)  42.5 us
  transfers between devices with their start and end apart: 6, of which 5 were waited for; matrix products, arithmetic and copies ran while one was open for 6% of the time, Pallas kernels for 0%

commit v1 on v0

v1 whole, which is shorter than its diff:
```python
import functools

import jax
import jax.numpy as jnp
from jax import lax
from jax.experimental import pallas as pl
from jax.experimental.pallas import tpu as pltpu
from jax.sharding import Mesh, PartitionSpec as P

HD = 128
ROWS = 128
HALF = ROWS // 2
GROUP = 8
CTX = 32
WINDOW = 2 * CTX
STAT = 16
LOG2E = 1.4426950408889634
SCALE = HD ** (-0.5)
FLOOR = -1e30

ZH, ZL, XH = "zh", "zl", "xh"
HEAD = ("y", "xl", "core")
Q_AXES = ("zl", "xh")
K_AXES = ("zh", "xh")

f32 = jnp.float32
bf16 = jnp.bfloat16


def q_block(pos_ref, s):
    return (pos_ref[0] * 4 + s // 2) * 2 + s % 2


def k_block(pos_ref, s):
    return ((s // 2) * 4 + pos_ref[1]) * 2 + s % 2


def time_of(block, offset):
    return jnp.where(
        offset < HALF, block * HALF + offset, (2 * CTX - 1 - block) * HALF + offset - HALF
    )


def split3(x):
    high = x.astype(bf16).astype(f32)
    rest = x - high
    mid = rest.astype(bf16).astype(f32)
    return high, mid, rest - mid


def stat_rows(a, b):
    row = lax.broadcasted_iota(jnp.int32, (STAT, ROWS), 0)
    out = jnp.zeros((STAT, ROWS), f32)
    for at, piece in enumerate(split3(a) + split3(b)):
        out = jnp.where(row == at, piece, out)
    return out.astype(bf16)


def stats_of(rows):
    rows = rows.astype(f32)
    return rows[0:1] + rows[1:2] + rows[2:3], rows[3:4] + rows[4:5] + rows[5:6]


def key_columns(pos_ref, kv_ref, s):
    offset = lax.broadcasted_iota(jnp.int32, (ROWS, ROWS), 0)
    times = time_of(k_block(pos_ref, s), offset)
    ep = kv_ref[s, 2 * ROWS : 2 * ROWS + STAT, :].astype(f32)[0:1]
    episodes = jnp.broadcast_to(ep, (ROWS, ROWS)).T
    return times, episodes


def query_rows(pos_ref, q_ref, s):
    offset = lax.broadcasted_iota(jnp.int32, (1, ROWS), 1)
    times = time_of(q_block(pos_ref, s), offset)
    ep = q_ref[s, ROWS : ROWS + STAT, :].astype(f32)[0:1]
    return times, ep - WINDOW


def pack_kernel(q_ref, k_ref, v_ref, ep_ref, qs_ref, kvs_ref):
    ep = jnp.broadcast_to(ep_ref[...].astype(f32), (STAT, ROWS)).astype(bf16)
    for s in range(GROUP):
        cols = slice((s % 2) * HD, (s % 2 + 1) * HD)
        qs_ref[s, 0:ROWS, :] = q_ref[:, cols]
        qs_ref[s, ROWS : ROWS + STAT, :] = ep
        kvs_ref[s, 0:ROWS, :] = k_ref[:, cols]
        kvs_ref[s, ROWS : 2 * ROWS, :] = v_ref[:, cols]
        kvs_ref[s, 2 * ROWS : 2 * ROWS + STAT, :] = ep


def forward_kernel(pos_ref, q_ref, kv_ref, os_ref, vt_ref, tk_ref, ek_ref):
    for s in range(GROUP):
        at = slice(s * ROWS, (s + 1) * ROWS)
        vt_ref[:, at] = kv_ref[s, ROWS : 2 * ROWS, :].T
        tk_ref[at, :], ek_ref[at, :] = key_columns(pos_ref, kv_ref, s)
    keys = kv_ref[:, 0:ROWS, :].reshape(GROUP * ROWS, HD)
    for s in range(0, GROUP, 2):
        qb = q_ref[s : s + 2, 0:ROWS, :].reshape(2 * ROWS, HD)
        st = lax.dot_general(keys, qb, (((1,), (1,)), ((), ())), preferred_element_type=f32)
        parts = []
        for u in range(2):
            tq, eq = query_rows(pos_ref, q_ref, s + u)
            seen = (tk_ref[...] <= tq) & (ek_ref[...] > eq)
            sc = jnp.where(seen, st[:, u * ROWS : (u + 1) * ROWS] * (SCALE * LOG2E), FLOOR)
            top = jnp.max(sc, axis=0, keepdims=True)
            p = jnp.exp2(sc - top)
            total = jnp.sum(p, axis=0, keepdims=True)
            parts.append(p.astype(bf16))
            os_ref[s + u, HD : HD + STAT, :] = stat_rows(top, total)
        o = jnp.dot(vt_ref[...], jnp.concatenate(parts, axis=1), preferred_element_type=f32)
        for u in range(2):
            os_ref[s + u, 0:HD, :] = o[:, u * ROWS : (u + 1) * ROWS].astype(bf16)


def combine_kernel(os_ref, da_ref, attn_ref, das_ref):
    for h in range(2):
        cols = slice(h * HD, (h + 1) * HD)
        stats = [stats_of(os_ref[2 * c + h, HD : HD + STAT, :]) for c in range(4)]
        top = functools.reduce(jnp.maximum, [m for m, _ in stats])
        weights = [jnp.exp2(m - top) for m, _ in stats]
        total = sum(w * t for w, (_, t) in zip(weights, stats))
        attn_t = sum(
            (w / total) * os_ref[2 * c + h, 0:HD, :].astype(f32) for c, w in enumerate(weights)
        )
        lse = top + jnp.log(total) * LOG2E
        low = attn_t.astype(bf16).astype(f32)
        attn_ref[:, cols] = low.T.astype(bf16)
        da = da_ref[:, cols]
        delta = jnp.sum(da.astype(f32).T * low, axis=0, keepdims=True)
        rows = stat_rows(lse, delta)
        for c in range(4):
            das_ref[2 * c + h, 0:ROWS, :] = da
            das_ref[2 * c + h, ROWS : ROWS + STAT, :] = rows


def backward_kernel(pos_ref, q_ref, kv_ref, das_ref, dqs_ref, dkvs_ref, dq_acc):
    total = GROUP * ROWS
    queries = q_ref[:, 0:ROWS, :].reshape(total, HD)
    d_attn = das_ref[:, 0:ROWS, :].reshape(total, HD)
    tq, eq, lse, delta = [], [], [], []
    for s in range(GROUP):
        t, e = query_rows(pos_ref, q_ref, s)
        a, b = stats_of(das_ref[s, ROWS : ROWS + STAT, :])
        tq.append(t)
        eq.append(e)
        lse.append(a)
        delta.append(b)
    for s in range(0, GROUP, 2):
        kb = kv_ref[s : s + 2, 0:ROWS, :].reshape(2 * ROWS, HD)
        vb = kv_ref[s : s + 2, ROWS : 2 * ROWS, :].reshape(2 * ROWS, HD)
        nt = (((1,), (1,)), ((), ()))
        st = lax.dot_general(kb, queries, nt, preferred_element_type=f32)
        dp = lax.dot_general(vb, d_attn, nt, preferred_element_type=f32)
        tk0, ek0 = key_columns(pos_ref, kv_ref, s)
        tk1, ek1 = key_columns(pos_ref, kv_ref, s + 1)
        tk = jnp.concatenate([tk0, tk1], axis=0)
        ek = jnp.concatenate([ek0, ek1], axis=0)
        p_low, ds_low = [], []
        for u in range(GROUP):
            at = slice(u * ROWS, (u + 1) * ROWS)
            seen = (tk <= tq[u]) & (ek > eq[u])
            p = jnp.where(seen, jnp.exp2(st[:, at] * (SCALE * LOG2E) - lse[u]), 0.0)
            p_low.append(p.astype(bf16))
            ds_low.append((p * (dp[:, at] - delta[u])).astype(bf16))
        probs = jnp.concatenate(p_low, axis=1)
        ds = jnp.concatenate(ds_low, axis=1)
        dv = jnp.dot(probs, d_attn, preferred_element_type=f32)
        dk = jnp.dot(ds, queries, preferred_element_type=f32)
        dq = jnp.dot(kb.T, ds, preferred_element_type=f32)
        if s == 0:
            dq_acc[...] = dq
        else:
            dq_acc[...] += dq
        for u in range(2):
            at = slice(u * ROWS, (u + 1) * ROWS)
            dkvs_ref[s + u, 0:ROWS, :] = dk[at].astype(bf16)
            dkvs_ref[s + u, ROWS : 2 * ROWS, :] = dv[at].astype(bf16)
    for s in range(GROUP):
        dqs_ref[s] = dq_acc[:, s * ROWS : (s + 1) * ROWS].astype(bf16)


def finish_kernel(dqs_ref, dkvs_ref, dq_ref, dk_ref, dv_ref):
    for h in range(2):
        cols = slice(h * HD, (h + 1) * HD)
        dq = sum(dqs_ref[2 * c + h].astype(f32) for c in range(4))
        dkv = sum(dkvs_ref[2 * c + h].astype(f32) for c in range(4))
        dq_ref[:, cols] = (dq * SCALE).T.astype(bf16)
        dk_ref[:, cols] = (dkv[0:ROWS] * SCALE).astype(bf16)
        dv_ref[:, cols] = dkv[ROWS : 2 * ROWS].astype(bf16)


VMEM = pl.BlockSpec(memory_space=pltpu.VMEM)
SMEM = pl.BlockSpec(memory_space=pltpu.SMEM)


def call(kernel, outs, args, scratch=(), flops=0, smem=0):
    moved = sum(a.size * a.dtype.itemsize for a in args) + sum(
        functools.reduce(lambda x, y: x * y, shape) * 2 for shape in outs
    )
    return pl.pallas_call(
        kernel,
        out_shape=[jax.ShapeDtypeStruct(shape, bf16) for shape in outs],
        in_specs=[SMEM] * smem + [VMEM] * (len(args) - smem),
        out_specs=[VMEM] * len(outs),
        scratch_shapes=list(scratch),
        compiler_params=pltpu.CompilerParams(vmem_limit_bytes=32 * 1024 * 1024),
        cost_estimate=pl.CostEstimate(flops=flops, bytes_accessed=moved, transcendentals=0),
    )(*args)


def on_device(queries, keys, values, episode, out_weight, d_out):
    rows, width = queries.shape
    total = GROUP * ROWS
    pos = jnp.stack([lax.axis_index(ZH), lax.axis_index(ZL)]).astype(jnp.int32)
    swap = functools.partial(lax.all_to_all, split_axis=0, concat_axis=0, tiled=True)
    d_out_all = lax.all_gather(d_out, HEAD, axis=0, tiled=True)
    q_slots, kv_slots = call(
        pack_kernel,
        [(GROUP, ROWS + STAT, HD), (GROUP, 2 * ROWS + STAT, HD)],
        (queries, keys, values, episode.reshape(1, rows)),
    )
    kv = swap(kv_slots, K_AXES)
    q = swap(q_slots, Q_AXES)
    (o_slots,) = call(
        forward_kernel,
        [(GROUP, HD + STAT, ROWS)],
        (pos, q, kv),
        [pltpu.VMEM((HD, total), bf16), pltpu.VMEM((total, ROWS), jnp.int32), pltpu.VMEM((total, ROWS), f32)],
        flops=4 * total * total * HD,
        smem=1,
    )
    o = swap(o_slots, Q_AXES)
    d_attn = lax.dot_general(
        d_out_all, out_weight, (((1,), (1,)), ((), ())), preferred_element_type=f32
    ).astype(bf16)
    attn, da_slots = call(
        combine_kernel, [(rows, width), (GROUP, ROWS + STAT, HD)], (o, d_attn)
    )
    partial = jnp.dot(attn, out_weight, preferred_element_type=f32)
    partial, da_slots = lax.optimization_barrier((partial, da_slots))
    mixed = lax.psum_scatter(partial, HEAD, scatter_dimension=0, tiled=True).astype(bf16)
    da = swap(da_slots, Q_AXES)
    dq_slots, dkv_slots = call(
        backward_kernel,
        [(GROUP, HD, ROWS), (GROUP, 2 * ROWS, HD)],
        (pos, q, kv, da),
        [pltpu.VMEM((HD, total), f32)],
        flops=10 * total * total * HD,
        smem=1,
    )
    dkv = swap(dkv_slots, K_AXES)
    dq = swap(dq_slots, Q_AXES)
    d_queries, d_keys, d_values = call(finish_kernel, [(rows, width)] * 3, (dq, dkv))
    return mixed, d_queries, d_keys, d_values


def solution(mesh):
    inner = Mesh(
        mesh.devices.reshape(4, 4, 2, 4, 2, 2), ("zh", "zl", "xh", "y", "xl", "core")
    )
    ctx = ("zh", "zl", "xh")
    block = P(ctx, HEAD)
    whole = P(ctx + HEAD, None)
    return jax.shard_map(
        on_device,
        mesh=inner,
        in_specs=(block, block, block, P(ctx), P(HEAD, None), whole),
        out_specs=(whole, block, block, block),
        check_vma=False,
    )
```

time: 721 us -> 182 us (0.25)
  the two profiles are of different devices: /device:TPU:4 before, /device:TPU:38 now
where the time goes in v1:
time: 182 us; the launch traced here: 181 us
  blocking collectives  90.9 us (50%)
  waiting for transfers between devices  34.1 us (19%)
  starting transfers between devices  21.9 us (12%)
  between operations  14.1 us (8%)
  Pallas kernels  9.91 us (5%)
  matrix products  4.48 us (2%)
  local copies, waits for them, and re-layouts  4.16 us (2%)
    all_to_all x1, blocking collectives, on_device(): dkv = swap(dkv_slots, K_AXES)  44.8 us
    all_to_all x1, waiting for transfers between devices, on_device(): kv = swap(kv_slots, K_AXES)  28.4 us
    all_to_all x1, blocking collectives, on_device(): da = swap(da_slots, Q_AXES)  16.5 us
    all_to_all x1, blocking collectives, on_device(): q = swap(q_slots, Q_AXES)  16.2 us
    all_to_all x1, starting transfers between devices, on_device(): kv = swap(kv_slots, K_AXES)  15.4 us
    all_to_all x1, blocking collectives, on_device(): dq = swap(dq_slots, Q_AXES)  13.4 us
    pallas_call x5, Pallas kernels, call(): pl.pallas_call(kernel, out_shape=[jax.ShapeDtypeStruct(shape, bf16) for s...  9.91 us
    all_to_all x1, starting transfers between devices, on_device(): o = swap(o_slots, Q_AXES)  6.51 us
  transfers between devices with their start and end apart: 4, of which 3 were waited for; matrix products, arithmetic and copies ran while one was open for 2% of the time, Pallas kernels for 5%

profile of v1, /device:TPU:38, one launch (start us, length us, event | category | flops | bytes accessed | tf_op | source)
XLA Modules:
  0.0 181.1 jit_solution(4024334413803177451)
XLA Ops:
  7.2 0.0 copy-start
  7.2 0.0 copy-start.2
  7.2 1.0 copy-done.2
  8.2 0.0 copy-start.3
  8.2 0.8 copy-done.3
  9.0 0.0 copy-start.4
  9.0 0.8 copy-done.4
  9.8 0.0 copy-start.5
  9.9 0.7 copy-done.5
  10.5 0.9 shard_map.93
  11.4 16.2 %all_to_all.30.q_ref = bf16[8,144,128]{2,1,0:T(8,128)(2,1)S(1)} all-to-all(bf16[8,144,128]{2,1,0:T(8,128)(2,1)S(1)} %get-tuple-element.15), channel_id=1, replica_groups=mesh['zh'=4,'zl'=4,'xh'=2,'y'=4,'xl'=2,'core'=2] {'zl','xh'}, dimensions={0} | all-to-all | bytes 589824 | tf_op jit(solution)/shard_map/all_to_all | solution.py:222
  27.7 15.4 %all-to-all-start.1 = ((bf16[8,272,128]{2,1,0:T(8,128)(2,1)}), bf16[8,272,128]{2,1,0:T(8,128)(2,1)S(1)}, u32[]{:S(2)}, u32[]{:S(2)}) async-start(bf16[8,272,128]{2,1,0:T(8,128)(2,1)} %get-tuple-element.16), calls=%async_computation.1 | async-start | bytes 1114112 | tf_op jit(solution)/shard_map/all_to_all | solution.py:221
  43.1 0.0 all-gather.2.cloned.1.call-start
  43.1 0.7 all-gather.2.cloned.1.call-update
  43.8 0.1 pad_add_fusion.pos_ref
  43.9 28.4 %all-to-all-done.1.kv_ref = bf16[8,272,128]{2,1,0:T(8,128)(2,1)S(1)} async-done(((bf16[8,272,128]{2,1,0:T(8,128)(2,1)}), bf16[8,272,128]{2,1,0:T(8,128)(2,1)S(1)}, u32[]{:S(2)}, u32[]{:S(2)}) %all-to-all-start.1) | async-done | bytes 557088 | tf_op jit(solution)/shard_map/all_to_all | solution.py:221
  72.3 4.2 %shard_map.94 = bf16[8,144,128]{2,1,0:T(8,128)(2,1)} custom-call(s32[2]{0:T(128)S(1)} %pad_add_fusion.pos_ref, bf16[8,144,128]{2,1,0:T(8,128)(2,1)S(1)} %all_to_all.30.q_ref, bf16[8,272,128]{2,1,0:T(8,128)(2,1)S(1)} %all-to-all-done.1.kv_ref), custom_call_target="tpu_custom_call" | custom-call | flops 536870912 | bytes 1146888 | tf_op jit(solution)/shard_map/pallas_call | solution.py:199
  76.5 6.5 %all-to-all-start.2 = ((bf16[8,144,128]{2,1,0:T(8,128)(2,1)}), bf16[8,144,128]{2,1,0:T(8,128)(2,1)S(1)}, u32[]{:S(2)}, u32[]{:S(2)}) async-start(bf16[8,144,128]{2,1,0:T(8,128)(2,1)} %shard_map.94), calls=%async_computation.2 | async-start | bytes 589824 | tf_op jit(solution)/shard_map/all_to_all | solution.py:231
  83.0 0.0 reduce-scatter.2.cloned.1.call-start
  83.0 4.7 %all-gather.2.cloned.1.call-done = bf16[128,4096]{1,0:T(8,128)(2,1)} async-done(((bf16[8,4096]{1,0:T(8,128)(2,1)}), bf16[128,4096]{1,0:T(8,128)(2,1)}) %all-gather.2.cloned.1.call-update) | async-done | bytes 1048592 | tf_op jit(solution)/shard_map/all_gather | solution.py:215
  87.7 0.0 copy-done
  87.7 2.7 %convolution_convert_fusion.da_ref = bf16[128,256]{1,0:T(8,128)(2,1)} fusion(bf16[128,4096]{1,0:T(8,128)(2,1)} %all-gather.2.cloned.1.call-done, bf16[256,4096]{1,0:T(8,128)(2,1)S(1)} %copy-done), kind=kOutput, calls=%fused_computation | convolution fusion | flops 268468224 | bytes 3211264 | tf_op jit(solution)/shard_map/dot_general | solution.py:232
  90.4 0.2 all-to-all-done.2.os_ref
  90.7 0.0 copy-start.1
  90.7 0.8 copy-done.1
  91.5 0.2 shard_map.95
  91.7 1.8 fusion
  93.5 0.0 reduce-scatter.2.cloned.1.call-update
  93.5 16.5 %all_to_all.31.das_ref = bf16[8,144,128]{2,1,0:T(8,128)(2,1)S(1)} all-to-all(bf16[8,144,128]{2,1,0:T(8,128)(2,1)S(1)} %get-tuple-element.20), channel_id=1, replica_groups=mesh['zh'=4,'zl'=4,'xh'=2,'y'=4,'xl'=2,'core'=2] {'zl','xh'}, dimensions={0} | all-to-all | bytes 589824 | tf_op jit(solution)/shard_map/all_to_all | solution.py:241
  110.0 3.8 %shard_map.96 = (bf16[8,128,128]{2,1,0:T(8,128)(2,1)S(1)}, bf16[8,256,128]{2,1,0:T(8,128)(2,1)S(1)}) custom-call(s32[2]{0:T(128)S(1)} %pad_add_fusion.pos_ref, bf16[8,144,128]{2,1,0:T(8,128)(2,1)S(1)} %all_to_all.30.q_ref, bf16[8,272,128]{2,1,0:T(8,128)(2,1)S(1)} %all-to-all-done.1.kv_ref, bf16[8,144,128]{2,1,0:T(8,128)(2,1)S(1)} %all_to_all.31.das_ref), custom_call_target="tpu_custom_call" | custom-call | flops 1342177280 | bytes 1933320 | tf_op jit(solution)/shard_map/pallas_call | solution.py:199
  113.8 13.4 %all_to_all.32.dqs_ref = bf16[8,128,128]{2,1,0:T(8,128)(2,1)S(1)} all-to-all(bf16[8,128,128]{2,1,0:T(8,128)(2,1)S(1)} %get-tuple-element.21), channel_id=1, replica_groups=mesh['zh'=4,'zl'=4,'xh'=2,'y'=4,'xl'=2,'core'=2] {'zl','xh'}, dimensions={0} | all-to-all | bytes 524288 | tf_op jit(solution)/shard_map/all_to_all | solution.py:251
  127.2 44.8 %all_to_all.33.dkvs_ref = bf16[8,256,128]{2,1,0:T(8,128)(2,1)S(1)} all-to-all(bf16[8,256,128]{2,1,0:T(8,128)(2,1)S(1)} %get-tuple-element.22), channel_id=1, replica_groups=mesh['zh'=4,'zl'=4,'xh'=2,'y'=4,'xl'=2,'core'=2] {'zh','xh'}, dimensions={0} | all-to-all | bytes 1048576 | tf_op jit(solution)/shard_map/all_to_all | solution.py:250
  172.0 0.8 shard_map.97
  172.8 0.0 reduce-scatter.2.cloned.1.call-done
  172.8 1.5 convert_element_type.7
Async XLA Ops:
  7.2 80.6 %copy-start = (bf16[256,4096]{1,0:T(8,128)(2,1)S(1)}, bf16[256,4096]{1,0:T(8,128)(2,1)}, u32[]{:S(2)}) copy-start(bf16[256,4096]{1,0:T(8,128)(2,1)} %param.10) | copy-start | bytes 6291460
  7.2 1.0 copy-start.2
  8.2 0.8 copy-start.3
  9.0 0.8 copy-start.4
  9.8 0.7 copy-start.5
  27.7 44.6 %all-to-all-start.1 = ((bf16[8,272,128]{2,1,0:T(8,128)(2,1)}), bf16[8,272,128]{2,1,0:T(8,128)(2,1)S(1)}, u32[]{:S(2)}, u32[]{:S(2)}) async-start(bf16[8,272,128]{2,1,0:T(8,128)(2,1)} %get-tuple-element.16), calls=%async_computation.1 | async-start | bytes 1114112 | tf_op jit(solution)/shard_map/all_to_all | solution.py:221
  43.1 44.7 %all-gather.2.cloned.1.call-start = ((), (), s32[]{:S(2)}) async-start(), calls=%async_computation.7 | async-start | bytes 1114112 | tf_op jit(solution)/shard_map/all_gather | solution.py:215
  76.5 14.1 %all-to-all-start.2 = ((bf16[8,144,128]{2,1,0:T(8,128)(2,1)}), bf16[8,144,128]{2,1,0:T(8,128)(2,1)S(1)}, u32[]{:S(2)}, u32[]{:S(2)}) async-start(bf16[8,144,128]{2,1,0:T(8,128)(2,1)} %shard_map.94), calls=%async_computation.2 | async-start | bytes 589824 | tf_op jit(solution)/shard_map/all_to_all | solution.py:231
  83.0 89.7 %reduce-scatter.2.cloned.1.call-start = ((), (), s32[]{:S(2)}) async-start(), calls=%async_computation.8 | async-start | bytes 2228224 | tf_op jit(solution)/shard_map/reduce_scatter | solution.py:240
  90.7 0.8 copy-start.1
Sparse Core Ops, SparseCore 0:
  46.0 41.6 all-gather.1
  93.6 71.7 reduce-scatter.1

commit v2 on v0

v2 whole, which is shorter than its diff:
```python
import functools

import jax
import jax.numpy as jnp
from jax import lax
from jax.experimental import pallas as pl
from jax.experimental.pallas import tpu as pltpu
from jax.sharding import Mesh, PartitionSpec as P

HD = 128
ROWS = 128
HALF = ROWS // 2
PIECE = 32
SHARES = 32
PLANES = 16
CTX = 32
WINDOW = 2 * CTX
STAT = 16
LOG2E = 1.4426950408889634
SCALE = HD ** (-0.5)
FLOOR = -1e30

AXES = ("z", "xh", "y", "xl", "core")
HEAD = ("y", "xl", "core")
TURN = ("z",) + HEAD
PLANE = ("xh",) + HEAD
S_AXES = ("xh", "xl")

f32 = jnp.float32
bf16 = jnp.bfloat16
NT = (((1,), (1,)), ((), ()))


def slot_of(place):
    return place % 8 * 2 + place // 8


def place_of(slot):
    return slot // 2 + slot % 2 * 8


def share(xh, y, xl, core):
    return ((xh * 4 + y) * 2 + xl) * 2 + core


def times_of(row, piece, plane):
    source = row // PIECE
    place = source % 2 * 8 + source // 4 % 4 * 2 + source // 2 % 2
    block = (place - plane + PLANES) % PLANES * 2 + source // 16
    offset = row % PIECE + piece % 2 * PIECE
    return jnp.where(piece < 2, block, 2 * CTX - 1 - block) * HALF + offset


def episodes_of(x_ref, at, group):
    lane = lax.broadcasted_iota(jnp.int32, (1, ROWS), 1) // PIECE
    out = jnp.zeros((1, ROWS), f32)
    for u in range(4):
        rows = x_ref[4 * group + u, 4 * PIECE : 4 * PIECE + STAT, :].astype(f32)
        out = jnp.where(lane == u, rows[at : at + 1], out)
    return out


def key_columns(pos_ref, x_ref, group):
    row = lax.broadcasted_iota(jnp.int32, (ROWS, ROWS), 0) + group * ROWS
    times = times_of(row, pos_ref[2] * 2 + pos_ref[1], pos_ref[3])
    return times, jnp.broadcast_to(episodes_of(x_ref, 1, group), (ROWS, ROWS)).T


def query_rows(pos_ref, x_ref, group):
    row = lax.broadcasted_iota(jnp.int32, (1, ROWS), 1) + group * ROWS
    times = times_of(row, pos_ref[0], pos_ref[3])
    return times, episodes_of(x_ref, 0, group) - WINDOW


def part(x_ref, at, first=0, count=SHARES):
    return x_ref[first : first + count, at * PIECE : (at + 1) * PIECE, :].reshape(count * PIECE, HD)


def prepare_kernel(q_ref, k_ref, v_ref, ep_ref, d_ref, qkv_out, d_out, ep_buf, d_buf, sems):
    copies = [
        pltpu.make_async_copy(q_ref, qkv_out.at[0:ROWS], sems.at[0]),
        pltpu.make_async_copy(k_ref, qkv_out.at[ROWS : 2 * ROWS], sems.at[1]),
        pltpu.make_async_copy(v_ref, qkv_out.at[2 * ROWS : 3 * ROWS], sems.at[2]),
        pltpu.make_async_copy(d_ref, d_buf, sems.at[3]),
        pltpu.make_async_copy(ep_ref, ep_buf, sems.at[4]),
    ]
    for copy in copies:
        copy.start()
    for copy in copies:
        copy.wait()
    ep = jnp.broadcast_to(ep_buf[...].astype(f32), (STAT, ROWS)).astype(bf16)
    qkv_out[3 * ROWS : 3 * ROWS + STAT] = jnp.concatenate([ep, ep], axis=1)
    for s in range(PLANES):
        d_out[s] = d_buf[...]


def pack_kernel(qkv_ref, da_ref, out_ref):
    ep = qkv_ref[3 * ROWS : 3 * ROWS + STAT, 0:ROWS].astype(f32)
    tiled = []
    for piece in range(4):
        own = ep[:, piece * PIECE : (piece + 1) * PIECE]
        tiled.append(jnp.concatenate([own] * 4, axis=1))
    row = lax.broadcasted_iota(jnp.int32, (STAT, ROWS), 0)
    for xh in range(2):
        for y in range(4):
            for xl in range(2):
                x = xh * 2 + xl
                both = jnp.where(row == 0, tiled[y], tiled[x]).astype(bf16)
                for core in range(2):
                    s = share(xh, y, xl, core)
                    cols = slice(core * HD, (core + 1) * HD)
                    q_rows = slice(y * PIECE, (y + 1) * PIECE)
                    out_ref[s, 0:PIECE, :] = qkv_ref[q_rows, cols]
                    out_ref[s, PIECE : 2 * PIECE, :] = da_ref[q_rows, cols]
                    for at in (1, 2):
                        k_rows = slice(at * ROWS + x * PIECE, at * ROWS + (x + 1) * PIECE)
                        out_ref[s, (at + 1) * PIECE : (at + 2) * PIECE, :] = qkv_ref[k_rows, cols]
                    out_ref[s, 4 * PIECE : 4 * PIECE + STAT, :] = both


def totals_kernel(pos_ref, x_ref, stat_ref, tk_ref, ek_ref):
    for g in range(8):
        at = slice(g * ROWS, (g + 1) * ROWS)
        tk_ref[at, :], ek_ref[at, :] = key_columns(pos_ref, x_ref, g)
    keys, values = part(x_ref, 2), part(x_ref, 3)
    row = lax.broadcasted_iota(jnp.int32, (8, ROWS), 0)
    for g in range(0, 8, 2):
        qb, db = part(x_ref, 0, 4 * g, 8), part(x_ref, 1, 4 * g, 8)
        st = lax.dot_general(keys, qb, NT, preferred_element_type=f32)
        dp = lax.dot_general(values, db, NT, preferred_element_type=f32)
        for u in range(2):
            tq, eq = query_rows(pos_ref, x_ref, g + u)
            at = slice(u * ROWS, (u + 1) * ROWS)
            seen = (tk_ref[...] <= tq) & (ek_ref[...] > eq)
            sc = jnp.where(seen, st[:, at] * (SCALE * LOG2E), FLOOR)
            top = jnp.max(sc, axis=0, keepdims=True)
            p = jnp.exp2(sc - top)
            total = jnp.sum(p, axis=0, keepdims=True)
            inner = jnp.sum(p * dp[:, at], axis=0, keepdims=True)
            rows = jnp.where(row == 0, top, jnp.where(row == 1, total, jnp.where(row == 2, inner, 0.0)))
            for c in range(4):
                stat_ref[c, :, (g + u) * ROWS : (g + u + 1) * ROWS] = rows


def backward_kernel(pos_ref, x_ref, stat_ref, oq_ref, grad_ref, dq_acc, o_acc):
    queries, d_attn = part(x_ref, 0), part(x_ref, 1)
    tops = [stat_ref[c, 0:1, :] for c in range(4)]
    top = functools.reduce(jnp.maximum, tops)
    weights = [jnp.exp2(t - top) for t in tops]
    norm = sum(w * stat_ref[c, 1:2, :] for c, w in enumerate(weights))
    lse = top + jnp.log(norm) * LOG2E
    delta = sum(w * stat_ref[c, 2:3, :] for c, w in enumerate(weights)) / norm
    rows = [query_rows(pos_ref, x_ref, g) for g in range(8)]
    for g in range(0, 8, 2):
        kb, vb = part(x_ref, 2, 4 * g, 8), part(x_ref, 3, 4 * g, 8)
        st = lax.dot_general(kb, queries, NT, preferred_element_type=f32)
        dp = lax.dot_general(vb, d_attn, NT, preferred_element_type=f32)
        tk0, ek0 = key_columns(pos_ref, x_ref, g)
        tk1, ek1 = key_columns(pos_ref, x_ref, g + 1)
        tk = jnp.concatenate([tk0, tk1], axis=0)
        ek = jnp.concatenate([ek0, ek1], axis=0)
        p_low, ds_low = [], []
        for u in range(8):
            at = slice(u * ROWS, (u + 1) * ROWS)
            tq, eq = rows[u]
            seen = (tk <= tq) & (ek > eq)
            p = jnp.where(seen, jnp.exp2(st[:, at] * (SCALE * LOG2E) - lse[:, at]), 0.0)
            p_low.append(p.astype(bf16))
            ds_low.append((p * (dp[:, at] - delta[:, at])).astype(bf16))
        probs = jnp.concatenate(p_low, axis=1)
        ds = jnp.concatenate(ds_low, axis=1)
        dv = jnp.dot(probs, d_attn, preferred_element_type=f32)
        dk = jnp.dot(ds, queries, preferred_element_type=f32)
        dq = jnp.dot(kb.T, ds, preferred_element_type=f32)
        o = jnp.dot(vb.T, probs, preferred_element_type=f32)
        if g == 0:
            dq_acc[...] = dq
            o_acc[...] = o
        else:
            dq_acc[...] += dq
            o_acc[...] += o
        for at, grad in ((0, dk), (1, dv)):
            grad_ref[4 * g : 4 * g + 8, at * PIECE : (at + 1) * PIECE, :] = grad.astype(
                bf16
            ).reshape(8, PIECE, HD)
    for g in range(8):
        at = slice(g * ROWS, (g + 1) * ROWS)
        four = slice(4 * g, 4 * g + 4)
        oq_ref[four, PIECE : 2 * PIECE, :] = dq_acc[:, at].T.astype(bf16).reshape(4, PIECE, HD)
        oq_ref[four, 0:PIECE, :] = o_acc[:, at].T.astype(bf16).reshape(4, PIECE, HD)


def queries_kernel(oq_ref, out_ref):
    for core in range(2):
        cols = slice(core * HD, (core + 1) * HD)
        for y in range(4):
            both = sum(oq_ref[share(x // 2, y, x % 2, core)].astype(f32) for x in range(4))
            rows = slice(y * PIECE, (y + 1) * PIECE)
            out_ref[rows, cols] = both[:PIECE].astype(bf16)
            rows = slice(ROWS + y * PIECE, ROWS + (y + 1) * PIECE)
            out_ref[rows, cols] = (both[PIECE:] * SCALE).astype(bf16)


def keys_kernel(grad_ref, out_ref):
    for core in range(2):
        cols = slice(core * HD, (core + 1) * HD)
        for x in range(4):
            both = sum(grad_ref[share(x // 2, y, x % 2, core)].astype(f32) for y in range(4))
            rows = slice(x * PIECE, (x + 1) * PIECE)
            out_ref[rows, cols] = (both[:PIECE] * SCALE).astype(bf16)
            rows = slice(ROWS + x * PIECE, ROWS + (x + 1) * PIECE)
            out_ref[rows, cols] = both[PIECE:].astype(bf16)


VMEM = pl.BlockSpec(memory_space=pltpu.VMEM)
SMEM = pl.BlockSpec(memory_space=pltpu.SMEM)


HBM = pl.BlockSpec(memory_space=pltpu.HBM)


def call(kernel, outs, args, scratch=(), flops=0, smem=0, space=VMEM, limit=32):
    size = lambda a: functools.reduce(lambda x, y: x * y, a.shape) * a.dtype.itemsize
    return pl.pallas_call(
        kernel,
        out_shape=outs,
        in_specs=[SMEM] * smem + [space] * (len(args) - smem),
        out_specs=[VMEM] * len(outs),
        scratch_shapes=list(scratch),
        compiler_params=pltpu.CompilerParams(vmem_limit_bytes=limit * 1024 * 1024),
        cost_estimate=pl.CostEstimate(
            flops=flops, bytes_accessed=sum(map(size, (*args, *outs))), transcendentals=0
        ),
    )(*args)


def turns():
    inside, across, there = [], [], []
    for z in range(PLANES):
        for g in range(PLANES):
            plane = place_of(g)
            at = slot_of((plane + z) % PLANES)
            inside.append((z * PLANES + g, z * PLANES + at))
            across.append((z * PLANES + at, plane * PLANES + at))
            there.append((z * PLANES + g, plane * PLANES + at))
    return inside, across, there, [(b, a) for a, b in there]


def on_device(queries, keys, values, episode, out_weight, d_out):
    rows, width = queries.shape
    total = SHARES * PIECE
    inside, across, there, back = turns()
    move = lambda x, pairs: lax.ppermute(x, TURN, pairs)
    swap = functools.partial(lax.all_to_all, split_axis=0, concat_axis=0, tiled=True)
    low = lambda *shape: jax.ShapeDtypeStruct(shape, bf16)
    pos = jnp.stack([lax.axis_index(a) for a in ("y", "xl", "xh", "z")]).astype(jnp.int32)
    qkv, d_slots = call(
        prepare_kernel,
        [low(3 * rows + STAT, width), low(PLANES, *d_out.shape)],
        (queries, keys, values, episode.reshape(1, rows), d_out),
        [
            pltpu.VMEM((1, rows), jnp.int32),
            pltpu.VMEM(d_out.shape, bf16),
            pltpu.SemaphoreType.DMA((5,)),
        ],
        space=HBM,
        limit=60,
    )
    qkv, d_slots = lax.optimization_barrier((move(qkv, inside), d_slots))
    qkv = move(qkv, across)
    d_out_all = swap(d_slots, HEAD)
    d_attn = lax.dot_general(
        d_out_all.reshape(rows, -1), out_weight, NT, preferred_element_type=f32
    ).astype(bf16)
    d_attn = move(d_attn, there)
    (slots,) = call(pack_kernel, [low(SHARES, 4 * PIECE + STAT, HD)], (qkv, d_attn))
    held = swap(slots, PLANE)
    (stats,) = call(
        totals_kernel,
        [jax.ShapeDtypeStruct((4, 8, total), f32)],
        (pos, held),
        [pltpu.VMEM((total, ROWS), jnp.int32), pltpu.VMEM((total, ROWS), f32)],
        flops=4 * total * total * HD,
        smem=1,
    )
    stats = swap(stats, S_AXES)
    oq_slots, grad_slots = call(
        backward_kernel,
        [low(SHARES, 2 * PIECE, HD), low(SHARES, 2 * PIECE, HD)],
        (pos, held, stats),
        [pltpu.VMEM((HD, total), f32)] * 2,
        flops=12 * total * total * HD,
        smem=1,
    )
    (own_q,) = call(queries_kernel, [low(2 * rows, width)], (swap(oq_slots, PLANE),))
    own_q = move(own_q, back)
    grad_parts, own_q = lax.optimization_barrier((swap(grad_slots, PLANE), own_q))
    (own_k,) = call(keys_kernel, [low(2 * rows, width)], (grad_parts,))
    own_k = move(own_k, back)
    partial = jnp.dot(own_q[:rows], out_weight, preferred_element_type=f32).astype(bf16)
    parts = swap(partial.reshape((PLANES,) + d_out.shape), HEAD)
    mixed = jnp.sum(parts.astype(f32), axis=0).astype(bf16)
    return mixed, own_q[rows:], own_k[:rows], own_k[rows:]


def solution(mesh):
    inner = Mesh(mesh.devices.reshape(16, 2, 4, 2, 2), AXES)
    ctx = ("z", "xh")
    block = P(ctx, HEAD)
    whole = P(ctx + HEAD, None)
    return jax.shard_map(
        on_device,
        mesh=inner,
        in_specs=(block, block, block, P(ctx), P(HEAD, None), whole),
        out_specs=(whole, block, block, block),
        check_vma=False,
    )
```

time: 721 us -> 165 us (0.23)
  the two profiles are of different devices: /device:TPU:4 before, /device:TPU:111 now
where the time goes in v2:
time: 165 us; the launch traced here: 164 us
  waiting for transfers between devices  62.6 us (38%)
  starting transfers between devices  59.2 us (36%)
  blocking collectives  23.7 us (14%)
  Pallas kernels  12.1 us (7%)
  matrix products  2.27 us (1%)
  other arithmetic  2.09 us (1%)
    ppermute x5, waiting for transfers between devices, on_device(): move = lambda x, pairs: lax.ppermute(x, TURN, pairs)  34.5 us
    ppermute x5, starting transfers between devices, on_device(): move = lambda x, pairs: lax.ppermute(x, TURN, pairs)  31.4 us
    all_to_all x1, blocking collectives, on_device(): swap(oq_slots, PLANE)  16.7 us
    all_to_all x1, waiting for transfers between devices, on_device(): held = swap(slots, PLANE)  14.9 us
    pallas_call x6, Pallas kernels, call(): pl.pallas_call(kernel, out_shape=outs, in_specs=[SMEM] * smem + [space] *...  12.1 us
    all_to_all x1, waiting for transfers between devices, on_device(): d_out_all = swap(d_slots, HEAD)  9.33 us
    all_to_all x1, starting transfers between devices, on_device(): held = swap(slots, PLANE)  8.05 us
    all_to_all x1, starting transfers between devices, on_device(): d_out_all = swap(d_slots, HEAD)  7.89 us
  transfers between devices with their start and end apart: 9, of which 7 were waited for; matrix products, arithmetic and copies ran while one was open for 1% of the time, Pallas kernels for 0%

profile of v2, /device:TPU:111, one launch (start us, length us, event | category | flops | bytes accessed | tf_op | source)
XLA Modules:
  0.0 164.1 jit_solution(8910526047770170489)
XLA Ops:
  0.6 0.0 copy-start
  0.6 2.3 %shard_map.93 = (bf16[400,256]{1,0:T(8,128)(2,1)}, bf16[16,8,4096]{2,1,0:T(8,128)(2,1)}) custom-call(bf16[128,256]{1,0:T(8,128)(2,1)} %q_ref.1, bf16[128,256]{1,0:T(8,128)(2,1)} %k_ref.1, bf16[128,256]{1,0:T(8,128)(2,1)} %v_ref.1, s32[1,128]{1,0:T(1,128)} %bitcast.12, bf16[8,4096]{1,0:T(8,128)(2,1)} %d_ref.1), custom_call_target="tpu_custom_call" | custom-call | bytes 1516032 | tf_op jit(solution)/shard_map/pallas_call | solution.py:224
  2.9 4.2 %collective-permute-start = (bf16[400,256]{1,0:T(8,128)(2,1)}, bf16[400,256]{1,0:T(8,128)(2,1)S(1)}, u32[]{:S(2)}, u32[]{:S(2)}) collective-permute-start(bf16[400,256]{1,0:T(8,128)(2,1)} %get-tuple-element.12), channel_id=1, source_target_pairs={{0,0},{1,1},{2,2},{3,3},{4,4},{5,5},{6,6},{7,7},{8,8},{9,9},{10,10... | collective-permute-start | bytes 614408 | tf_op jit(solution)/shard_map/ppermute | solution.py:253
  7.1 4.8 %collective-permute-done = bf16[400,256]{1,0:T(8,128)(2,1)S(1)} collective-permute-done((bf16[400,256]{1,0:T(8,128)(2,1)}, bf16[400,256]{1,0:T(8,128)(2,1)S(1)}, u32[]{:S(2)}, u32[]{:S(2)}) %collective-permute-start) | collective-permute-done | bytes 204832 | tf_op jit(solution)/shard_map/ppermute | solution.py:253
  11.9 7.9 %all-to-all-start = ((bf16[16,8,4096]{2,1,0:T(8,128)(2,1)}), bf16[16,8,4096]{2,1,0:T(8,128)(2,1)S(1)}, u32[]{:S(2)}, u32[]{:S(2)}) async-start(bf16[16,8,4096]{2,1,0:T(8,128)(2,1)} %get-tuple-element.15), calls=%async_computation | async-start | bytes 2097152 | tf_op jit(solution)/shard_map/all_to_all | solution.py:271
  19.8 4.2 %collective-permute-start.1 = (bf16[400,256]{1,0:T(8,128)(2,1)S(1)}, bf16[400,256]{1,0:T(8,128)(2,1)S(1)}, u32[]{:S(2)}, u32[]{:S(2)}) collective-permute-start(bf16[400,256]{1,0:T(8,128)(2,1)S(1)} %collective-permute-done), channel_id=1, source_target_pairs={{0,0},{1,257},{2,34},{3,291},{4,68},{5,325},{6,102},{7,359},{8,136... | collective-permute-start | bytes 614408 | tf_op jit(solution)/shard_map/ppermute | solution.py:253
  24.0 9.3 %all-to-all-done = bf16[16,8,4096]{2,1,0:T(8,128)(2,1)S(1)} async-done(((bf16[16,8,4096]{2,1,0:T(8,128)(2,1)}), bf16[16,8,4096]{2,1,0:T(8,128)(2,1)S(1)}, u32[]{:S(2)}, u32[]{:S(2)}) %all-to-all-start) | async-done | bytes 1048608 | tf_op jit(solution)/shard_map/all_to_all | solution.py:271
  33.3 0.0 copy-done
  33.3 0.8 convolution_convert_fusion.1
  34.2 15.0 %collective-permute-start.2 = (bf16[128,256]{1,0:T(8,128)(2,1)S(1)}, bf16[128,256]{1,0:T(8,128)(2,1)S(1)}, u32[]{:S(2)}, u32[]{:S(2)}) collective-permute-start(bf16[128,256]{1,0:T(8,128)(2,1)S(1)} %convolution_convert_fusion.1), channel_id=1, source_target_pairs={{0,0},{1,257},{2,34},{3,291},{4,68},{5,325},{6,102},{7,359},{8,136... | collective-permute-start | bytes 196616 | tf_op jit(solution)/shard_map/ppermute | solution.py:253
  49.1 0.0 collective-permute-done.1.qkv_ref
  49.2 1.3 collective-permute-done.2.da_ref
  50.5 1.2 shard_map.94
  51.6 8.0 %all-to-all-start.1 = ((bf16[32,144,128]{2,1,0:T(8,128)(2,1)}), bf16[32,144,128]{2,1,0:T(8,128)(2,1)S(1)}, u32[]{:S(2)}, u32[]{:S(2)}) async-start(bf16[32,144,128]{2,1,0:T(8,128)(2,1)} %shard_map.94), calls=%async_computation.1 | async-start | bytes 2359296 | tf_op jit(solution)/shard_map/all_to_all | solution.py:277
  59.7 0.1 pad_add_fusion.pos_ref
  59.8 14.9 %all-to-all-done.1.x_ref = bf16[32,144,128]{2,1,0:T(8,128)(2,1)S(1)} async-done(((bf16[32,144,128]{2,1,0:T(8,128)(2,1)}), bf16[32,144,128]{2,1,0:T(8,128)(2,1)S(1)}, u32[]{:S(2)}, u32[]{:S(2)}) %all-to-all-start.1) | async-done | bytes 1179680 | tf_op jit(solution)/shard_map/all_to_all | solution.py:277
  74.6 3.5 %shard_map.95 = f32[4,8,1024]{2,1,0:T(8,128)S(1)} custom-call(s32[4]{0:T(128)S(1)} %pad_add_fusion.pos_ref, bf16[32,144,128]{2,1,0:T(8,128)(2,1)S(1)} %all-to-all-done.1.x_ref), custom_call_target="tpu_custom_call" | custom-call | flops 536870912 | bytes 1310736 | tf_op jit(solution)/shard_map/pallas_call | solution.py:224
  78.1 7.0 %all_to_all.30.stat_ref = f32[4,8,1024]{2,1,0:T(8,128)S(1)} all-to-all(f32[4,8,1024]{2,1,0:T(8,128)S(1)} %shard_map.95), channel_id=1, replica_groups=mesh['z'=16,'xh'=2,'y'=4,'xl'=2,'core'=2] {'xh','xl'}, dimensions={0} | all-to-all | bytes 262144 | tf_op jit(solution)/shard_map/all_to_all | solution.py:286
  85.1 5.0 %shard_map.96 = (bf16[32,64,128]{2,1,0:T(8,128)(2,1)S(1)}, bf16[32,64,128]{2,1,0:T(8,128)(2,1)S(1)}) custom-call(s32[4]{0:T(128)S(1)} %pad_add_fusion.pos_ref, bf16[32,144,128]{2,1,0:T(8,128)(2,1)S(1)} %all-to-all-done.1.x_ref, f32[4,8,1024]{2,1,0:T(8,128)S(1)} %all_to_all.30.stat_ref), custom_call_target="tpu_custom_call" | custom-call | flops 1610612736 | bytes 2359312 | tf_op jit(solution)/shard_map/pallas_call | solution.py:224
  90.2 0.0 copy-start.1
  90.2 16.7 %all_to_all.31.oq_ref = bf16[32,64,128]{2,1,0:T(8,128)(2,1)S(1)} all-to-all(bf16[32,64,128]{2,1,0:T(8,128)(2,1)S(1)} %get-tuple-element.17), channel_id=1, replica_groups=mesh['z'=16,'xh'=2,'y'=4,'xl'=2,'core'=2] {'xh','y','xl','core'}, dimensions={0} | all-to-all | bytes 1048576 | tf_op jit(solution)/shard_map/all_to_all | solution.py:295
  106.9 0.0 copy-done.1
  106.9 7.7 %all-to-all-start.3 = ((bf16[32,64,128]{2,1,0:T(8,128)(2,1)}), bf16[32,64,128]{2,1,0:T(8,128)(2,1)S(1)}, u32[]{:S(2)}, u32[]{:S(2)}) async-start(bf16[32,64,128]{2,1,0:T(8,128)(2,1)} %copy-done.1), calls=%async_computation.3 | async-start | bytes 1048576 | tf_op jit(solution)/shard_map/all_to_all | solution.py:297
  114.6 0.1 shard_map.97
  114.7 5.3 %collective-permute-start.3 = (bf16[256,256]{1,0:T(8,128)(2,1)S(1)}, bf16[256,256]{1,0:T(8,128)(2,1)S(1)}, u32[]{:S(2)}, u32[]{:S(2)}) collective-permute-start(bf16[256,256]{1,0:T(8,128)(2,1)S(1)} %shard_map.97), channel_id=1, source_target_pairs={{0,0},{257,1},{34,2},{291,3},{68,4},{325,5},{102,6},{359,7},{136,8... | collective-permute-start | bytes 393224 | tf_op jit(solution)/shard_map/ppermute | solution.py:253
  120.0 4.0 %all-to-all-done.3.grad_ref = bf16[32,64,128]{2,1,0:T(8,128)(2,1)S(1)} async-done(((bf16[32,64,128]{2,1,0:T(8,128)(2,1)}), bf16[32,64,128]{2,1,0:T(8,128)(2,1)S(1)}, u32[]{:S(2)}, u32[]{:S(2)}) %all-to-all-start.3) | async-done | bytes 524320 | tf_op jit(solution)/shard_map/all_to_all | solution.py:297
  123.9 12.1 %collective-permute-done.3 = bf16[256,256]{1,0:T(8,128)(2,1)S(1)} collective-permute-done((bf16[256,256]{1,0:T(8,128)(2,1)S(1)}, bf16[256,256]{1,0:T(8,128)(2,1)S(1)}, u32[]{:S(2)}, u32[]{:S(2)}) %collective-permute-start.3) | collective-permute-done | bytes 131104 | tf_op jit(solution)/shard_map/ppermute | solution.py:253
  136.0 1.4 fusion
  137.4 4.2 %all-to-all-start.5 = ((bf16[16,8,4096]{2,1,0:T(8,128)(2,1)}), bf16[16,8,4096]{2,1,0:T(8,128)(2,1)}, u32[]{:S(2)}, u32[]{:S(2)}) async-start(bf16[16,8,4096]{2,1,0:T(8,128)(2,1)} %fusion), calls=%async_computation.5 | async-start | bytes 2097152 | tf_op jit(solution)/shard_map/all_to_all | solution.py:301
  141.7 0.1 shard_map.98
  141.7 2.7 %collective-permute-start.4 = (bf16[256,256]{1,0:T(8,128)(2,1)S(1)}, bf16[256,256]{1,0:T(8,128)(2,1)S(1)}, u32[]{:S(2)}, u32[]{:S(2)}) collective-permute-start(bf16[256,256]{1,0:T(8,128)(2,1)S(1)} %shard_map.98), channel_id=1, source_target_pairs={{0,0},{257,1},{34,2},{291,3},{68,4},{325,5},{102,6},{359,7},{136,8... | collective-permute-start | bytes 393224 | tf_op jit(solution)/shard_map/ppermute | solution.py:253
  144.4 0.6 slice.13
  145.1 16.4 %collective-permute-done.4 = bf16[256,256]{1,0:T(8,128)(2,1)S(1)} collective-permute-done((bf16[256,256]{1,0:T(8,128)(2,1)S(1)}, bf16[256,256]{1,0:T(8,128)(2,1)S(1)}, u32[]{:S(2)}, u32[]{:S(2)}) %collective-permute-start.4) | collective-permute-done | bytes 131104 | tf_op jit(solution)/shard_map/ppermute | solution.py:253
  161.4 0.7 fusion.3
  162.1 0.0 all-to-all-done.5
  162.1 2.0 %reduce_sum.12 = bf16[8,4096]{1,0:T(8,128)(2,1)} reduce(bf16[16,8,4096]{2,1,0:T(8,128)(2,1)} %all-to-all-done.5, bf16[]{:T(256)} %constant.20.clone.1), dimensions={0}, to_apply=%region_0.0 | reduce | flops 491520 | bytes 1114114 | tf_op jit(solution)/shard_map/reduce_sum | solution.py:302
Async XLA Ops:
  0.6 32.7 %copy-start = (bf16[256,4096]{1,0:T(8,128)(2,1)S(1)}, bf16[256,4096]{1,0:T(8,128)(2,1)}, u32[]{:S(2)}) copy-start(bf16[256,4096]{1,0:T(8,128)(2,1)} %param.10) | copy-start | bytes 6291460
  2.9 8.9 %collective-permute-start = (bf16[400,256]{1,0:T(8,128)(2,1)}, bf16[400,256]{1,0:T(8,128)(2,1)S(1)}, u32[]{:S(2)}, u32[]{:S(2)}) collective-permute-start(bf16[400,256]{1,0:T(8,128)(2,1)} %get-tuple-element.12), channel_id=1, source_target_pairs={{0,0},{1,1},{2,2},{3,3},{4,4},{5,5},{6,6},{7,7},{8,8},{9,9},{10,10... | collective-permute-start | bytes 614408 | tf_op jit(solution)/shard_map/ppermute | solution.py:253
  11.9 21.5 %all-to-all-start = ((bf16[16,8,4096]{2,1,0:T(8,128)(2,1)}), bf16[16,8,4096]{2,1,0:T(8,128)(2,1)S(1)}, u32[]{:S(2)}, u32[]{:S(2)}) async-start(bf16[16,8,4096]{2,1,0:T(8,128)(2,1)} %get-tuple-element.15), calls=%async_computation | async-start | bytes 2097152 | tf_op jit(solution)/shard_map/all_to_all | solution.py:271
  19.8 29.4 %collective-permute-start.1 = (bf16[400,256]{1,0:T(8,128)(2,1)S(1)}, bf16[400,256]{1,0:T(8,128)(2,1)S(1)}, u32[]{:S(2)}, u32[]{:S(2)}) collective-permute-start(bf16[400,256]{1,0:T(8,128)(2,1)S(1)} %collective-permute-done), channel_id=1, source_target_pairs={{0,0},{1,257},{2,34},{3,291},{4,68},{5,325},{6,102},{7,359},{8,136... | collective-permute-start | bytes 614408 | tf_op jit(solution)/shard_map/ppermute | solution.py:253
  34.2 16.3 %collective-permute-start.2 = (bf16[128,256]{1,0:T(8,128)(2,1)S(1)}, bf16[128,256]{1,0:T(8,128)(2,1)S(1)}, u32[]{:S(2)}, u32[]{:S(2)}) collective-permute-start(bf16[128,256]{1,0:T(8,128)(2,1)S(1)} %convolution_convert_fusion.1), channel_id=1, source_target_pairs={{0,0},{1,257},{2,34},{3,291},{4,68},{5,325},{6,102},{7,359},{8,136... | collective-permute-start | bytes 196616 | tf_op jit(solution)/shard_map/ppermute | solution.py:253
  51.6 23.0 %all-to-all-start.1 = ((bf16[32,144,128]{2,1,0:T(8,128)(2,1)}), bf16[32,144,128]{2,1,0:T(8,128)(2,1)S(1)}, u32[]{:S(2)}, u32[]{:S(2)}) async-start(bf16[32,144,128]{2,1,0:T(8,128)(2,1)} %shard_map.94), calls=%async_computation.1 | async-start | bytes 2359296 | tf_op jit(solution)/shard_map/all_to_all | solution.py:277
  90.2 16.8 %copy-start.1 = (bf16[32,64,128]{2,1,0:T(8,128)(2,1)}, bf16[32,64,128]{2,1,0:T(8,128)(2,1)S(1)}, u32[]{:S(2)}) copy-start(bf16[32,64,128]{2,1,0:T(8,128)(2,1)S(1)} %get-tuple-element.16) | copy-start | bytes 1572868
  106.9 17.0 %all-to-all-start.3 = ((bf16[32,64,128]{2,1,0:T(8,128)(2,1)}), bf16[32,64,128]{2,1,0:T(8,128)(2,1)S(1)}, u32[]{:S(2)}, u32[]{:S(2)}) async-start(bf16[32,64,128]{2,1,0:T(8,128)(2,1)} %copy-done.1), calls=%async_computation.3 | async-start | bytes 1048576 | tf_op jit(solution)/shard_map/all_to_all | solution.py:297
  114.7 21.3 %collective-permute-start.3 = (bf16[256,256]{1,0:T(8,128)(2,1)S(1)}, bf16[256,256]{1,0:T(8,128)(2,1)S(1)}, u32[]{:S(2)}, u32[]{:S(2)}) collective-permute-start(bf16[256,256]{1,0:T(8,128)(2,1)S(1)} %shard_map.97), channel_id=1, source_target_pairs={{0,0},{257,1},{34,2},{291,3},{68,4},{325,5},{102,6},{359,7},{136,8... | collective-permute-start | bytes 393224 | tf_op jit(solution)/shard_map/ppermute | solution.py:253
  137.4 24.7 %all-to-all-start.5 = ((bf16[16,8,4096]{2,1,0:T(8,128)(2,1)}), bf16[16,8,4096]{2,1,0:T(8,128)(2,1)}, u32[]{:S(2)}, u32[]{:S(2)}) async-start(bf16[16,8,4096]{2,1,0:T(8,128)(2,1)} %fusion), calls=%async_computation.5 | async-start | bytes 2097152 | tf_op jit(solution)/shard_map/all_to_all | solution.py:301
  141.7 19.7 %collective-permute-start.4 = (bf16[256,256]{1,0:T(8,128)(2,1)S(1)}, bf16[256,256]{1,0:T(8,128)(2,1)S(1)}, u32[]{:S(2)}, u32[]{:S(2)}) collective-permute-start(bf16[256,256]{1,0:T(8,128)(2,1)S(1)} %shard_map.98), channel_id=1, source_target_pairs={{0,0},{257,1},{34,2},{291,3},{68,4},{325,5},{102,6},{359,7},{136,8... | collective-permute-start | bytes 393224 | tf_op jit(solution)/shard_map/ppermute | solution.py:253

commit v3 on v2

v3 whole, which is shorter than its diff:
```python
import functools

import jax
import jax.numpy as jnp
from jax import lax
from jax.experimental import pallas as pl
from jax.experimental.pallas import tpu as pltpu
from jax.sharding import Mesh, PartitionSpec as P

HD = 128
ROWS = 128
HALF = ROWS // 2
PIECE = 32
SHARES = 32
PLANES = 16
CTX = 32
WINDOW = 2 * CTX
STAT = 16
LOG2E = 1.4426950408889634
SCALE = HD ** (-0.5)
FLOOR = -1e30

AXES = ("z", "xh", "y", "xl", "core")
HEAD = ("y", "xl", "core")
TURN = ("z",) + HEAD
PLANE = ("xh",) + HEAD

f32 = jnp.float32
bf16 = jnp.bfloat16
NT = (((1,), (1,)), ((), ()))


def slot_of(place):
    return place % 8 * 2 + place // 8


def place_of(slot):
    return slot // 2 + slot % 2 * 8


def share(xh, y, xl, core):
    return ((xh * 4 + y) * 2 + xl) * 2 + core


def times_of(row, piece, plane):
    source = row // PIECE
    place = source % 2 * 8 + source // 4 % 4 * 2 + source // 2 % 2
    block = (place - plane + PLANES) % PLANES * 2 + source // 16
    offset = row % PIECE + piece % 2 * PIECE
    return jnp.where(piece < 2, block, 2 * CTX - 1 - block) * HALF + offset


def episodes_of(x_ref, at, group):
    lane = lax.broadcasted_iota(jnp.int32, (1, ROWS), 1) // PIECE
    out = jnp.zeros((1, ROWS), f32)
    for u in range(4):
        rows = x_ref[4 * group + u, 3 * PIECE : 3 * PIECE + STAT, :].astype(f32)
        out = jnp.where(lane == u, rows[at : at + 1], out)
    return out


def split3(x):
    high = x.astype(bf16).astype(f32)
    rest = x - high
    mid = rest.astype(bf16).astype(f32)
    return high, mid, rest - mid


def stat_rows(a, b):
    row = lax.broadcasted_iota(jnp.int32, (STAT, ROWS), 0)
    out = jnp.zeros((STAT, ROWS), f32)
    for at, piece in enumerate(split3(a) + split3(b)):
        out = jnp.where(row == at, piece, out)
    return out


def stats_of(rows):
    return rows[0:1] + rows[1:2] + rows[2:3], rows[3:4] + rows[4:5] + rows[5:6]


def tile(rows, at):
    own = rows[:, at * PIECE : (at + 1) * PIECE]
    return jnp.concatenate([own] * 4, axis=1).astype(bf16)


def merge(pieces):
    lane = lax.broadcasted_iota(jnp.int32, (STAT, ROWS), 1) // PIECE
    out = jnp.zeros((STAT, ROWS), f32)
    for u, piece in enumerate(pieces):
        out = jnp.where(lane == u, piece.astype(f32), out)
    return out


def key_columns(pos_ref, x_ref, group):
    row = lax.broadcasted_iota(jnp.int32, (ROWS, ROWS), 0) + group * ROWS
    times = times_of(row, pos_ref[2] * 2 + pos_ref[1], pos_ref[3])
    return times, jnp.broadcast_to(episodes_of(x_ref, 1, group), (ROWS, ROWS)).T


def query_rows(pos_ref, x_ref, group):
    row = lax.broadcasted_iota(jnp.int32, (1, ROWS), 1) + group * ROWS
    times = times_of(row, pos_ref[0], pos_ref[3])
    return times, episodes_of(x_ref, 0, group) - WINDOW


def part(x_ref, at, first=0, count=SHARES):
    return x_ref[first : first + count, at * PIECE : (at + 1) * PIECE, :].reshape(count * PIECE, HD)


def prepare_kernel(q_ref, k_ref, v_ref, ep_ref, qkv_out, ep_buf, sems):
    copies = [
        pltpu.make_async_copy(q_ref, qkv_out.at[0:ROWS], sems.at[0]),
        pltpu.make_async_copy(k_ref, qkv_out.at[ROWS : 2 * ROWS], sems.at[1]),
        pltpu.make_async_copy(v_ref, qkv_out.at[2 * ROWS : 3 * ROWS], sems.at[2]),
        pltpu.make_async_copy(ep_ref, ep_buf, sems.at[3]),
    ]
    for copy in copies:
        copy.start()
    for copy in copies:
        copy.wait()
    ep = jnp.broadcast_to(ep_buf[...].astype(f32), (STAT, ROWS)).astype(bf16)
    qkv_out[3 * ROWS : 3 * ROWS + STAT] = jnp.concatenate([ep, ep], axis=1)


def repeat_kernel(d_ref, d_out, d_buf, sem):
    copy = pltpu.make_async_copy(d_ref, d_buf, sem)
    copy.start()
    copy.wait()
    for s in range(PLANES):
        d_out[s] = d_buf[...]


def pack_kernel(qkv_ref, out_ref):
    ep = qkv_ref[3 * ROWS : 3 * ROWS + STAT, 0:ROWS].astype(f32)
    tiled = []
    for piece in range(4):
        own = ep[:, piece * PIECE : (piece + 1) * PIECE]
        tiled.append(jnp.concatenate([own] * 4, axis=1))
    row = lax.broadcasted_iota(jnp.int32, (STAT, ROWS), 0)
    for xh in range(2):
        for y in range(4):
            for xl in range(2):
                x = xh * 2 + xl
                both = jnp.where(row == 0, tiled[y], tiled[x]).astype(bf16)
                for core in range(2):
                    s = share(xh, y, xl, core)
                    cols = slice(core * HD, (core + 1) * HD)
                    q_rows = slice(y * PIECE, (y + 1) * PIECE)
                    out_ref[s, 0:PIECE, :] = qkv_ref[q_rows, cols]
                    for at in (1, 2):
                        k_rows = slice(at * ROWS + x * PIECE, at * ROWS + (x + 1) * PIECE)
                        out_ref[s, at * PIECE : (at + 1) * PIECE, :] = qkv_ref[k_rows, cols]
                    out_ref[s, 3 * PIECE : 3 * PIECE + STAT, :] = both


def forward_kernel(pos_ref, x_ref, o_ref, tk_ref, ek_ref, vt_ref):
    for g in range(8):
        at = slice(g * ROWS, (g + 1) * ROWS)
        tk_ref[at, :], ek_ref[at, :] = key_columns(pos_ref, x_ref, g)
        vt_ref[:, at] = part(x_ref, 2, 4 * g, 4).T
    keys = part(x_ref, 1)
    for g in range(0, 8, 2):
        qb = part(x_ref, 0, 4 * g, 8)
        st = lax.dot_general(keys, qb, NT, preferred_element_type=f32)
        low = []
        for u in range(2):
            tq, eq = query_rows(pos_ref, x_ref, g + u)
            at = slice(u * ROWS, (u + 1) * ROWS)
            seen = (tk_ref[...] <= tq) & (ek_ref[...] > eq)
            sc = jnp.where(seen, st[:, at] * (SCALE * LOG2E), FLOOR)
            top = jnp.max(sc, axis=0, keepdims=True)
            p = jnp.exp2(sc - top)
            rows = stat_rows(top, jnp.sum(p, axis=0, keepdims=True))
            low.append(p.astype(bf16))
            for j in range(4):
                o_ref[4 * (g + u) + j, PIECE : PIECE + STAT, :] = tile(rows, j)
        o = jnp.dot(vt_ref[...], jnp.concatenate(low, axis=1), preferred_element_type=f32)
        for u in range(2):
            four = slice(4 * (g + u), 4 * (g + u) + 4)
            out = o[:, u * ROWS : (u + 1) * ROWS].T.astype(bf16)
            o_ref[four, 0:PIECE, :] = out.reshape(4, PIECE, HD)


def combine_kernel(o_ref, da_ref, attn_ref, das_ref):
    for core in range(2):
        cols = slice(core * HD, (core + 1) * HD)
        tops, sums, parts = [], [], []
        for x in range(4):
            slots = [share(x // 2, y, x % 2, core) for y in range(4)]
            top, total = stats_of(merge([o_ref[s, PIECE : PIECE + STAT, :] for s in slots]))
            tops.append(top)
            sums.append(total)
            parts.append(jnp.concatenate([o_ref[s, 0:PIECE, :] for s in slots], axis=0).astype(f32))
        top = functools.reduce(jnp.maximum, tops)
        weights = [jnp.exp2(t - top) for t in tops]
        total = sum(w * t for w, t in zip(weights, sums))
        low = sum(
            jnp.broadcast_to(w / total, (ROWS, ROWS)).T * o for w, o in zip(weights, parts)
        ).astype(bf16)
        attn_ref[:, cols] = low
        da = da_ref[:, cols]
        delta = jnp.sum((da.astype(f32) * low.astype(f32)).T, axis=0, keepdims=True)
        rows = stat_rows(top + jnp.log(total) * LOG2E, delta)
        for y in range(4):
            own = tile(rows, y)
            for x in range(4):
                s = share(x // 2, y, x % 2, core)
                das_ref[s, 0:PIECE, :] = da[y * PIECE : (y + 1) * PIECE]
                das_ref[s, PIECE : PIECE + STAT, :] = own


def backward_kernel(pos_ref, x_ref, d_ref, grad_ref, dq_acc):
    queries, d_attn = part(x_ref, 0), part(d_ref, 0)
    rows, stats = [], []
    for g in range(8):
        rows.append(query_rows(pos_ref, x_ref, g))
        stats.append(
            stats_of(merge([d_ref[4 * g + u, PIECE : PIECE + STAT, :] for u in range(4)]))
        )
    for g in range(0, 8, 2):
        kb, vb = part(x_ref, 1, 4 * g, 8), part(x_ref, 2, 4 * g, 8)
        st = lax.dot_general(kb, queries, NT, preferred_element_type=f32)
        dp = lax.dot_general(vb, d_attn, NT, preferred_element_type=f32)
        tk0, ek0 = key_columns(pos_ref, x_ref, g)
        tk1, ek1 = key_columns(pos_ref, x_ref, g + 1)
        tk = jnp.concatenate([tk0, tk1], axis=0)
        ek = jnp.concatenate([ek0, ek1], axis=0)
        p_low, ds_low = [], []
        for u in range(8):
            at = slice(u * ROWS, (u + 1) * ROWS)
            (tq, eq), (lse, delta) = rows[u], stats[u]
            seen = (tk <= tq) & (ek > eq)
            p = jnp.where(seen, jnp.exp2(st[:, at] * (SCALE * LOG2E) - lse), 0.0)
            p_low.append(p.astype(bf16))
            ds_low.append((p * (dp[:, at] - delta)).astype(bf16))
        probs = jnp.concatenate(p_low, axis=1)
        ds = jnp.concatenate(ds_low, axis=1)
        dv = jnp.dot(probs, d_attn, preferred_element_type=f32)
        dk = jnp.dot(ds, queries, preferred_element_type=f32)
        dq = jnp.dot(kb.T, ds, preferred_element_type=f32)
        if g == 0:
            dq_acc[...] = dq
        else:
            dq_acc[...] += dq
        for at, grad in ((1, dk), (2, dv)):
            grad_ref[4 * g : 4 * g + 8, at * PIECE : (at + 1) * PIECE, :] = grad.astype(
                bf16
            ).reshape(8, PIECE, HD)
    for g in range(8):
        at = slice(g * ROWS, (g + 1) * ROWS)
        four = slice(4 * g, 4 * g + 4)
        grad_ref[four, 0:PIECE, :] = dq_acc[:, at].T.astype(bf16).reshape(4, PIECE, HD)


def grads_kernel(grad_ref, out_ref):
    for core in range(2):
        cols = slice(core * HD, (core + 1) * HD)
        for i in range(4):
            over_x = [grad_ref[share(x // 2, i, x % 2, core), 0:PIECE].astype(f32) for x in range(4)]
            rows = slice(i * PIECE, (i + 1) * PIECE)
            out_ref[rows, cols] = (sum(over_x) * SCALE).astype(bf16)
            over_y = [grad_ref[share(i // 2, y, i % 2, core), PIECE:].astype(f32) for y in range(4)]
            both = sum(over_y)
            rows = slice(ROWS + i * PIECE, ROWS + (i + 1) * PIECE)
            out_ref[rows, cols] = (both[:PIECE] * SCALE).astype(bf16)
            rows = slice(2 * ROWS + i * PIECE, 2 * ROWS + (i + 1) * PIECE)
            out_ref[rows, cols] = both[PIECE:].astype(bf16)


VMEM = pl.BlockSpec(memory_space=pltpu.VMEM)
SMEM = pl.BlockSpec(memory_space=pltpu.SMEM)


HBM = pl.BlockSpec(memory_space=pltpu.HBM)


def call(kernel, outs, args, scratch=(), flops=0, smem=0, space=VMEM, limit=32):
    size = lambda a: functools.reduce(lambda x, y: x * y, a.shape) * a.dtype.itemsize
    return pl.pallas_call(
        kernel,
        out_shape=outs,
        in_specs=[SMEM] * smem + [space] * (len(args) - smem),
        out_specs=[VMEM] * len(outs),
        scratch_shapes=list(scratch),
        compiler_params=pltpu.CompilerParams(vmem_limit_bytes=limit * 1024 * 1024),
        cost_estimate=pl.CostEstimate(
            flops=flops, bytes_accessed=sum(map(size, (*args, *outs))), transcendentals=0
        ),
    )(*args)


def turns():
    inside, across, there = [], [], []
    for z in range(PLANES):
        for g in range(PLANES):
            plane = place_of(g)
            at = slot_of((plane + z) % PLANES)
            inside.append((z * PLANES + g, z * PLANES + at))
            across.append((z * PLANES + at, plane * PLANES + at))
            there.append((z * PLANES + g, plane * PLANES + at))
    return inside, across, there, [(b, a) for a, b in there]


def on_device(queries, keys, values, episode, out_weight, d_out):
    rows, width = queries.shape
    total = SHARES * PIECE
    inside, across, there, back = turns()
    move = lambda x, pairs: lax.ppermute(x, TURN, pairs)
    swap = functools.partial(lax.all_to_all, split_axis=0, concat_axis=0, tiled=True)
    low = lambda *shape: jax.ShapeDtypeStruct(shape, bf16)
    pos = jnp.stack([lax.axis_index(a) for a in ("y", "xl", "xh", "z")]).astype(jnp.int32)
    (qkv,) = call(
        prepare_kernel,
        [low(3 * rows + STAT, width)],
        (queries, keys, values, episode.reshape(1, rows)),
        [pltpu.VMEM((1, rows), jnp.int32), pltpu.SemaphoreType.DMA((4,))],
        space=HBM,
        limit=60,
    )
    (d_slots,) = call(
        repeat_kernel,
        [low(PLANES, *d_out.shape)],
        (d_out,),
        [pltpu.VMEM(d_out.shape, bf16), pltpu.SemaphoreType.DMA],
        space=HBM,
        limit=60,
    )
    qkv, d_slots = lax.optimization_barrier((move(qkv, inside), d_slots))
    qkv = move(qkv, across)
    d_out_all = swap(d_slots, HEAD)
    d_attn = lax.dot_general(
        d_out_all.reshape(rows, -1), out_weight, NT, preferred_element_type=f32
    ).astype(bf16)
    qkv, d_attn = lax.optimization_barrier((qkv, d_attn))
    d_attn = move(d_attn, there)
    (slots,) = call(pack_kernel, [low(SHARES, 3 * PIECE + STAT, HD)], (qkv,))
    held = swap(slots, PLANE)
    (o_slots,) = call(
        forward_kernel,
        [low(SHARES, PIECE + STAT, HD)],
        (pos, held),
        [
            pltpu.VMEM((total, ROWS), jnp.int32),
            pltpu.VMEM((total, ROWS), f32),
            pltpu.VMEM((HD, total), bf16),
        ],
        flops=4 * total * total * HD,
        smem=1,
    )
    o_slots, d_attn = lax.optimization_barrier((o_slots, d_attn))
    attn, da_slots = call(
        combine_kernel,
        [low(rows, width), low(SHARES, PIECE + STAT, HD)],
        (swap(o_slots, PLANE), d_attn),
    )
    attn = move(attn, back)
    (grad_slots,) = call(
        backward_kernel,
        [low(SHARES, 3 * PIECE, HD)],
        (pos, held, swap(da_slots, PLANE)),
        [pltpu.VMEM((HD, total), f32)],
        flops=10 * total * total * HD,
        smem=1,
    )
    grad_parts, attn = lax.optimization_barrier((swap(grad_slots, PLANE), attn))
    (grads,) = call(grads_kernel, [low(3 * rows, width)], (grad_parts,))
    grads = move(grads, back)
    partial = jnp.dot(attn, out_weight, preferred_element_type=f32).astype(bf16)
    parts = swap(partial.reshape((PLANES,) + d_out.shape), HEAD)
    mixed = jnp.sum(parts.astype(f32), axis=0).astype(bf16)
    return mixed, grads[:rows], grads[rows : 2 * rows], grads[2 * rows :]


def solution(mesh):
    inner = Mesh(mesh.devices.reshape(16, 2, 4, 2, 2), AXES)
    ctx = ("z", "xh")
    block = P(ctx, HEAD)
    whole = P(ctx + HEAD, None)
    return jax.shard_map(
        on_device,
        mesh=inner,
        in_specs=(block, block, block, P(ctx), P(HEAD, None), whole),
        out_specs=(whole, block, block, block),
        check_vma=False,
    )
```

time: 165 us -> 163 us (0.988)
  the two profiles are of different devices: /device:TPU:111 before, /device:TPU:107 now
where the time goes in v3:
time: 163 us; the launch traced here: 162 us
  starting transfers between devices  60.2 us (37%)
  waiting for transfers between devices  53.3 us (33%)
  blocking collectives  27.7 us (17%)
  Pallas kernels  14.1 us (9%)
  matrix products  2.28 us (1%)
  other arithmetic  2.09 us (1%)
    ppermute x5, waiting for transfers between devices, on_device(): move = lambda x, pairs: lax.ppermute(x, TURN, pairs)  37 us
    ppermute x5, starting transfers between devices, on_device(): move = lambda x, pairs: lax.ppermute(x, TURN, pairs)  25.8 us
    all_to_all x1, starting transfers between devices, on_device(): held = swap(slots, PLANE)  15.4 us
    pallas_call x7, Pallas kernels, call(): pl.pallas_call(kernel, out_shape=outs, in_specs=[SMEM] * smem + [space] *...  14.1 us
    all_to_all x1, blocking collectives, on_device(): swap(da_slots, PLANE)  14.1 us
    all_to_all x1, blocking collectives, on_device(): swap(o_slots, PLANE)  13.6 us
    all_to_all x1, waiting for transfers between devices, on_device(): d_out_all = swap(d_slots, HEAD)  8.74 us
    all_to_all x1, starting transfers between devices, on_device(): d_out_all = swap(d_slots, HEAD)  7.6 us
  transfers between devices with their start and end apart: 9, of which 6 were waited for; matrix products, arithmetic and copies ran while one was open for 1% of the time, Pallas kernels for 4%

profile of v3, /device:TPU:107, one launch (start us, length us, event | category | flops | bytes accessed | tf_op | source)
XLA Modules:
  0.0 162.0 jit_solution(4639910325079535437)
XLA Ops:
  0.6 0.0 copy-start
  0.6 1.8 %shard_map.93 = bf16[400,256]{1,0:T(8,128)(2,1)} custom-call(bf16[128,256]{1,0:T(8,128)(2,1)} %q_ref.1, bf16[128,256]{1,0:T(8,128)(2,1)} %k_ref.1, bf16[128,256]{1,0:T(8,128)(2,1)} %v_ref.1, s32[1,128]{1,0:T(1,128)} %bitcast.13), custom_call_target="tpu_custom_call" | custom-call | bytes 401920 | tf_op jit(solution)/shard_map/pallas_call | solution.py:279
  2.4 3.9 %collective-permute-start = (bf16[400,256]{1,0:T(8,128)(2,1)}, bf16[400,256]{1,0:T(8,128)(2,1)}, u32[]{:S(2)}, u32[]{:S(2)}) collective-permute-start(bf16[400,256]{1,0:T(8,128)(2,1)} %shard_map.93), channel_id=1, source_target_pairs={{0,0},{1,1},{2,2},{3,3},{4,4},{5,5},{6,6},{7,7},{8,8},{9,9},{10,10... | collective-permute-start | bytes 614408 | tf_op jit(solution)/shard_map/ppermute | solution.py:308
  6.3 1.9 %shard_map.94 = bf16[16,8,4096]{2,1,0:T(8,128)(2,1)} custom-call(bf16[8,4096]{1,0:T(8,128)(2,1)} %d_ref.1), custom_call_target="tpu_custom_call" | custom-call | bytes 1114112 | tf_op jit(solution)/shard_map/pallas_call | solution.py:279
  8.2 3.2 %collective-permute-done = bf16[400,256]{1,0:T(8,128)(2,1)} collective-permute-done((bf16[400,256]{1,0:T(8,128)(2,1)}, bf16[400,256]{1,0:T(8,128)(2,1)}, u32[]{:S(2)}, u32[]{:S(2)}) %collective-permute-start) | collective-permute-done | bytes 204832 | tf_op jit(solution)/shard_map/ppermute | solution.py:308
  11.5 7.6 %all-to-all-start = ((bf16[16,8,4096]{2,1,0:T(8,128)(2,1)}), bf16[16,8,4096]{2,1,0:T(8,128)(2,1)S(1)}, u32[]{:S(2)}, u32[]{:S(2)}) async-start(bf16[16,8,4096]{2,1,0:T(8,128)(2,1)} %shard_map.94), calls=%async_computation | async-start | bytes 2097152 | tf_op jit(solution)/shard_map/all_to_all | solution.py:330
  19.1 4.8 %collective-permute-start.1 = (bf16[400,256]{1,0:T(8,128)(2,1)}, bf16[400,256]{1,0:T(8,128)(2,1)S(1)}, u32[]{:S(2)}, u32[]{:S(2)}) collective-permute-start(bf16[400,256]{1,0:T(8,128)(2,1)} %collective-permute-done), channel_id=1, source_target_pairs={{0,0},{1,257},{2,34},{3,291},{4,68},{5,325},{6,102},{7,359},{8,136... | collective-permute-start | bytes 614408 | tf_op jit(solution)/shard_map/ppermute | solution.py:308
  23.9 8.7 %all-to-all-done = bf16[16,8,4096]{2,1,0:T(8,128)(2,1)S(1)} async-done(((bf16[16,8,4096]{2,1,0:T(8,128)(2,1)}), bf16[16,8,4096]{2,1,0:T(8,128)(2,1)S(1)}, u32[]{:S(2)}, u32[]{:S(2)}) %all-to-all-start) | async-done | bytes 1048608 | tf_op jit(solution)/shard_map/all_to_all | solution.py:330
  32.6 0.0 copy-done
  32.6 0.8 convolution_convert_fusion.1
  33.5 0.7 collective-permute-done.1.qkv_ref
  34.2 1.0 shard_map.95
  35.2 15.4 %all-to-all-start.1 = ((bf16[32,112,128]{2,1,0:T(8,128)(2,1)}), bf16[32,112,128]{2,1,0:T(8,128)(2,1)S(1)}, u32[]{:S(2)}, u32[]{:S(2)}) async-start(bf16[32,112,128]{2,1,0:T(8,128)(2,1)} %shard_map.95), calls=%async_computation.1 | async-start | bytes 1835008 | tf_op jit(solution)/shard_map/all_to_all | solution.py:337
  50.7 8.8 %collective-permute-start.2 = (bf16[128,256]{1,0:T(8,128)(2,1)S(1)}, bf16[128,256]{1,0:T(8,128)(2,1)S(1)}, u32[]{:S(2)}, u32[]{:S(2)}) collective-permute-start(bf16[128,256]{1,0:T(8,128)(2,1)S(1)} %convolution_convert_fusion.1), channel_id=1, source_target_pairs={{0,0},{1,257},{2,34},{3,291},{4,68},{5,325},{6,102},{7,359},{8,136... | collective-permute-start | bytes 196616 | tf_op jit(solution)/shard_map/ppermute | solution.py:308
  59.5 0.1 pad_add_fusion.pos_ref
  59.6 7.5 %all-to-all-done.1.x_ref = bf16[32,112,128]{2,1,0:T(8,128)(2,1)S(1)} async-done(((bf16[32,112,128]{2,1,0:T(8,128)(2,1)}), bf16[32,112,128]{2,1,0:T(8,128)(2,1)S(1)}, u32[]{:S(2)}, u32[]{:S(2)}) %all-to-all-start.1) | async-done | bytes 917536 | tf_op jit(solution)/shard_map/all_to_all | solution.py:337
  67.1 4.3 %shard_map.96 = bf16[32,48,128]{2,1,0:T(8,128)(2,1)S(1)} custom-call(s32[4]{0:T(128)S(1)} %pad_add_fusion.pos_ref, bf16[32,112,128]{2,1,0:T(8,128)(2,1)S(1)} %all-to-all-done.1.x_ref), custom_call_target="tpu_custom_call" | custom-call | flops 536870912 | bytes 1310736 | tf_op jit(solution)/shard_map/pallas_call | solution.py:279
  71.4 0.0 collective-permute-done.2.da_ref
  71.4 13.6 %all_to_all.30.o_ref = bf16[32,48,128]{2,1,0:T(8,128)(2,1)S(1)} all-to-all(bf16[32,48,128]{2,1,0:T(8,128)(2,1)S(1)} %shard_map.96), channel_id=1, replica_groups=mesh['z'=16,'xh'=2,'y'=4,'xl'=2,'core'=2] {'xh','y','xl','core'}, dimensions={0} | all-to-all | bytes 786432 | tf_op jit(solution)/shard_map/all_to_all | solution.py:354
  85.0 0.4 shard_map.97
  85.4 14.1 %all_to_all.31.d_ref = bf16[32,48,128]{2,1,0:T(8,128)(2,1)S(1)} all-to-all(bf16[32,48,128]{2,1,0:T(8,128)(2,1)S(1)} %get-tuple-element.20), channel_id=1, replica_groups=mesh['z'=16,'xh'=2,'y'=4,'xl'=2,'core'=2] {'xh','y','xl','core'}, dimensions={0} | all-to-all | bytes 786432 | tf_op jit(solution)/shard_map/all_to_all | solution.py:360
  99.5 4.6 %shard_map.98 = bf16[32,96,128]{2,1,0:T(8,128)(2,1)S(1)} custom-call(s32[4]{0:T(128)S(1)} %pad_add_fusion.pos_ref, bf16[32,112,128]{2,1,0:T(8,128)(2,1)S(1)} %all-to-all-done.1.x_ref, bf16[32,48,128]{2,1,0:T(8,128)(2,1)S(1)} %all_to_all.31.d_ref), custom_call_target="tpu_custom_call" | custom-call | flops 1342177280 | bytes 2097168 | tf_op jit(solution)/shard_map/pallas_call | solution.py:279
  104.0 0.0 copy-start.1
  104.1 0.9 copy-done.1
  105.0 7.1 %all-to-all-start.4 = ((bf16[32,96,128]{2,1,0:T(8,128)(2,1)}), bf16[32,96,128]{2,1,0:T(8,128)(2,1)S(1)}, u32[]{:S(2)}, u32[]{:S(2)}) async-start(bf16[32,96,128]{2,1,0:T(8,128)(2,1)} %copy-done.1), calls=%async_computation.4 | async-start | bytes 1572864 | tf_op jit(solution)/shard_map/all_to_all | solution.py:365
  112.1 4.8 %collective-permute-start.3 = (bf16[128,256]{1,0:T(8,128)(2,1)S(1)}, bf16[128,256]{1,0:T(8,128)(2,1)S(1)}, u32[]{:S(2)}, u32[]{:S(2)}) collective-permute-start(bf16[128,256]{1,0:T(8,128)(2,1)S(1)} %get-tuple-element.21), channel_id=1, source_target_pairs={{0,0},{257,1},{34,2},{291,3},{68,4},{325,5},{102,6},{359,7},{136,8... | collective-permute-start | bytes 196616 | tf_op jit(solution)/shard_map/ppermute | solution.py:308
  116.9 13.6 %collective-permute-done.3 = bf16[128,256]{1,0:T(8,128)(2,1)S(1)} collective-permute-done((bf16[128,256]{1,0:T(8,128)(2,1)S(1)}, bf16[128,256]{1,0:T(8,128)(2,1)S(1)}, u32[]{:S(2)}, u32[]{:S(2)}) %collective-permute-start.3) | collective-permute-done | bytes 65568 | tf_op jit(solution)/shard_map/ppermute | solution.py:308
  130.5 0.0 all-to-all-done.4.grad_ref
  130.5 1.4 fusion
  132.0 4.2 %all-to-all-start.5 = ((bf16[16,8,4096]{2,1,0:T(8,128)(2,1)}), bf16[16,8,4096]{2,1,0:T(8,128)(2,1)}, u32[]{:S(2)}, u32[]{:S(2)}) async-start(bf16[16,8,4096]{2,1,0:T(8,128)(2,1)} %fusion), calls=%async_computation.5 | async-start | bytes 2097152 | tf_op jit(solution)/shard_map/all_to_all | solution.py:369
  136.2 0.1 shard_map.99
  136.3 3.4 %collective-permute-start.4 = (bf16[384,256]{1,0:T(8,128)(2,1)S(1)}, bf16[384,256]{1,0:T(8,128)(2,1)S(1)}, u32[]{:S(2)}, u32[]{:S(2)}) collective-permute-start(bf16[384,256]{1,0:T(8,128)(2,1)S(1)} %shard_map.99), channel_id=1, source_target_pairs={{0,0},{257,1},{34,2},{291,3},{68,4},{325,5},{102,6},{359,7},{136,8... | collective-permute-start | bytes 589832 | tf_op jit(solution)/shard_map/ppermute | solution.py:308
  139.8 19.5 %collective-permute-done.4 = bf16[384,256]{1,0:T(8,128)(2,1)S(1)} collective-permute-done((bf16[384,256]{1,0:T(8,128)(2,1)S(1)}, bf16[384,256]{1,0:T(8,128)(2,1)S(1)}, u32[]{:S(2)}, u32[]{:S(2)}) %collective-permute-start.4) | collective-permute-done | bytes 196640 | tf_op jit(solution)/shard_map/ppermute | solution.py:308
  159.3 0.7 fusion.2
  160.0 0.0 all-to-all-done.5
  160.0 2.0 %reduce_sum.12 = bf16[8,4096]{1,0:T(8,128)(2,1)} reduce(bf16[16,8,4096]{2,1,0:T(8,128)(2,1)} %all-to-all-done.5, bf16[]{:T(256)} %constant.20.clone.1), dimensions={0}, to_apply=%region_0.0 | reduce | flops 491520 | bytes 1114114 | tf_op jit(solution)/shard_map/reduce_sum | solution.py:370
Async XLA Ops:
  0.6 32.0 %copy-start = (bf16[256,4096]{1,0:T(8,128)(2,1)S(1)}, bf16[256,4096]{1,0:T(8,128)(2,1)}, u32[]{:S(2)}) copy-start(bf16[256,4096]{1,0:T(8,128)(2,1)} %param.10) | copy-start | bytes 6291460
  2.4 9.1 %collective-permute-start = (bf16[400,256]{1,0:T(8,128)(2,1)}, bf16[400,256]{1,0:T(8,128)(2,1)}, u32[]{:S(2)}, u32[]{:S(2)}) collective-permute-start(bf16[400,256]{1,0:T(8,128)(2,1)} %shard_map.93), channel_id=1, source_target_pairs={{0,0},{1,1},{2,2},{3,3},{4,4},{5,5},{6,6},{7,7},{8,8},{9,9},{10,10... | collective-permute-start | bytes 614408 | tf_op jit(solution)/shard_map/ppermute | solution.py:308
  11.5 21.2 %all-to-all-start = ((bf16[16,8,4096]{2,1,0:T(8,128)(2,1)}), bf16[16,8,4096]{2,1,0:T(8,128)(2,1)S(1)}, u32[]{:S(2)}, u32[]{:S(2)}) async-start(bf16[16,8,4096]{2,1,0:T(8,128)(2,1)} %shard_map.94), calls=%async_computation | async-start | bytes 2097152 | tf_op jit(solution)/shard_map/all_to_all | solution.py:330
  19.1 15.1 %collective-permute-start.1 = (bf16[400,256]{1,0:T(8,128)(2,1)}, bf16[400,256]{1,0:T(8,128)(2,1)S(1)}, u32[]{:S(2)}, u32[]{:S(2)}) collective-permute-start(bf16[400,256]{1,0:T(8,128)(2,1)} %collective-permute-done), channel_id=1, source_target_pairs={{0,0},{1,257},{2,34},{3,291},{4,68},{5,325},{6,102},{7,359},{8,136... | collective-permute-start | bytes 614408 | tf_op jit(solution)/shard_map/ppermute | solution.py:308
  35.2 31.9 %all-to-all-start.1 = ((bf16[32,112,128]{2,1,0:T(8,128)(2,1)}), bf16[32,112,128]{2,1,0:T(8,128)(2,1)S(1)}, u32[]{:S(2)}, u32[]{:S(2)}) async-start(bf16[32,112,128]{2,1,0:T(8,128)(2,1)} %shard_map.95), calls=%async_computation.1 | async-start | bytes 1835008 | tf_op jit(solution)/shard_map/all_to_all | solution.py:337
  50.7 20.7 %collective-permute-start.2 = (bf16[128,256]{1,0:T(8,128)(2,1)S(1)}, bf16[128,256]{1,0:T(8,128)(2,1)S(1)}, u32[]{:S(2)}, u32[]{:S(2)}) collective-permute-start(bf16[128,256]{1,0:T(8,128)(2,1)S(1)} %convolution_convert_fusion.1), channel_id=1, source_target_pairs={{0,0},{1,257},{2,34},{3,291},{4,68},{5,325},{6,102},{7,359},{8,136... | collective-permute-start | bytes 196616 | tf_op jit(solution)/shard_map/ppermute | solution.py:308
  104.0 0.9 copy-start.1
  105.0 25.6 %all-to-all-start.4 = ((bf16[32,96,128]{2,1,0:T(8,128)(2,1)}), bf16[32,96,128]{2,1,0:T(8,128)(2,1)S(1)}, u32[]{:S(2)}, u32[]{:S(2)}) async-start(bf16[32,96,128]{2,1,0:T(8,128)(2,1)} %copy-done.1), calls=%async_computation.4 | async-start | bytes 1572864 | tf_op jit(solution)/shard_map/all_to_all | solution.py:365
  112.1 18.4 %collective-permute-start.3 = (bf16[128,256]{1,0:T(8,128)(2,1)S(1)}, bf16[128,256]{1,0:T(8,128)(2,1)S(1)}, u32[]{:S(2)}, u32[]{:S(2)}) collective-permute-start(bf16[128,256]{1,0:T(8,128)(2,1)S(1)} %get-tuple-element.21), channel_id=1, source_target_pairs={{0,0},{257,1},{34,2},{291,3},{68,4},{325,5},{102,6},{359,7},{136,8... | collective-permute-start | bytes 196616 | tf_op jit(solution)/shard_map/ppermute | solution.py:308
  132.0 28.0 %all-to-all-start.5 = ((bf16[16,8,4096]{2,1,0:T(8,128)(2,1)}), bf16[16,8,4096]{2,1,0:T(8,128)(2,1)}, u32[]{:S(2)}, u32[]{:S(2)}) async-start(bf16[16,8,4096]{2,1,0:T(8,128)(2,1)} %fusion), calls=%async_computation.5 | async-start | bytes 2097152 | tf_op jit(solution)/shard_map/all_to_all | solution.py:369
  136.3 22.9 %collective-permute-start.4 = (bf16[384,256]{1,0:T(8,128)(2,1)S(1)}, bf16[384,256]{1,0:T(8,128)(2,1)S(1)}, u32[]{:S(2)}, u32[]{:S(2)}) collective-permute-start(bf16[384,256]{1,0:T(8,128)(2,1)S(1)} %shard_map.99), channel_id=1, source_target_pairs={{0,0},{257,1},{34,2},{291,3},{68,4},{325,5},{102,6},{359,7},{136,8... | collective-permute-start | bytes 589832 | tf_op jit(solution)/shard_map/ppermute | solution.py:308

commit v4 on v3

--- a/solution.py
+++ b/solution.py
@@ -45,7 +45,7 @@
 def times_of(row, piece, plane):
     source = row // PIECE
     place = source % 2 * 8 + source // 4 % 4 * 2 + source // 2 % 2
-    block = (place - plane + PLANES) % PLANES * 2 + source // 16
+    block = (place ^ plane) * 2 + source // 16
     offset = row % PIECE + piece % 2 * PIECE
     return jnp.where(piece < 2, block, 2 * CTX - 1 - block) * HALF + offset
 
@@ -294,7 +294,7 @@
     for z in range(PLANES):
         for g in range(PLANES):
             plane = place_of(g)
-            at = slot_of((plane + z) % PLANES)
+            at = slot_of(plane ^ z)
             inside.append((z * PLANES + g, z * PLANES + at))
             across.append((z * PLANES + at, plane * PLANES + at))
             there.append((z * PLANES + g, plane * PLANES + at))

time: 163 us -> 160 us (0.982)
  the two profiles are of different devices: /device:TPU:107 before, /device:TPU:183 now
where the time goes in v4:
time: 160 us; the launch traced here: 159 us
  waiting for transfers between devices  61.1 us (38%)
  starting transfers between devices  49.2 us (31%)
  blocking collectives  28.4 us (18%)
  Pallas kernels  13.6 us (8%)
  matrix products  2.28 us (1%)
  other arithmetic  2.09 us (1%)
    ppermute x5, waiting for transfers between devices, on_device(): move = lambda x, pairs: lax.ppermute(x, TURN, pairs)  42.6 us
    ppermute x5, starting transfers between devices, on_device(): move = lambda x, pairs: lax.ppermute(x, TURN, pairs)  17.6 us
    all_to_all x1, blocking collectives, on_device(): swap(o_slots, PLANE)  14.3 us
    all_to_all x1, blocking collectives, on_device(): swap(da_slots, PLANE)  14.1 us
    pallas_call x7, Pallas kernels, call(): pl.pallas_call(kernel, out_shape=outs, in_specs=[SMEM] * smem + [space] *...  13.6 us
    all_to_all x1, waiting for transfers between devices, on_device(): d_out_all = swap(d_slots, HEAD)  11.7 us
    all_to_all x1, starting transfers between devices, on_device(): held = swap(slots, PLANE)  11.3 us
    all_to_all x1, starting transfers between devices, on_device(): grad_parts, attn = lax.optimization_barrier((swap(grad_slots, PLANE), attn))  7.96 us
  transfers between devices with their start and end apart: 9, of which 6 were waited for; matrix products, arithmetic and copies ran while one was open for 1% of the time, Pallas kernels for 4%

profile of v4, /device:TPU:183, one launch (start us, length us, event | category | flops | bytes accessed | tf_op | source)
XLA Modules:
  0.0 159.1 jit_solution(14035717676309301978)
XLA Ops:
  0.6 0.0 copy-start
  0.6 1.8 %shard_map.93 = bf16[400,256]{1,0:T(8,128)(2,1)} custom-call(bf16[128,256]{1,0:T(8,128)(2,1)} %q_ref.1, bf16[128,256]{1,0:T(8,128)(2,1)} %k_ref.1, bf16[128,256]{1,0:T(8,128)(2,1)} %v_ref.1, s32[1,128]{1,0:T(1,128)} %bitcast.13), custom_call_target="tpu_custom_call" | custom-call | bytes 401920 | tf_op jit(solution)/shard_map/pallas_call | solution.py:279
  2.4 2.2 %collective-permute-start = (bf16[400,256]{1,0:T(8,128)(2,1)}, bf16[400,256]{1,0:T(8,128)(2,1)}, u32[]{:S(2)}, u32[]{:S(2)}) collective-permute-start(bf16[400,256]{1,0:T(8,128)(2,1)} %shard_map.93), channel_id=1, source_target_pairs={{0,0},{1,1},{2,2},{3,3},{4,4},{5,5},{6,6},{7,7},{8,8},{9,9},{10,10... | collective-permute-start | bytes 614408 | tf_op jit(solution)/shard_map/ppermute | solution.py:308
  4.7 1.9 %shard_map.94 = bf16[16,8,4096]{2,1,0:T(8,128)(2,1)} custom-call(bf16[8,4096]{1,0:T(8,128)(2,1)} %d_ref.1), custom_call_target="tpu_custom_call" | custom-call | bytes 1114112 | tf_op jit(solution)/shard_map/pallas_call | solution.py:279
  6.6 6.4 %collective-permute-done = bf16[400,256]{1,0:T(8,128)(2,1)} collective-permute-done((bf16[400,256]{1,0:T(8,128)(2,1)}, bf16[400,256]{1,0:T(8,128)(2,1)}, u32[]{:S(2)}, u32[]{:S(2)}) %collective-permute-start) | collective-permute-done | bytes 204832 | tf_op jit(solution)/shard_map/ppermute | solution.py:308
  13.0 6.9 %all-to-all-start = ((bf16[16,8,4096]{2,1,0:T(8,128)(2,1)}), bf16[16,8,4096]{2,1,0:T(8,128)(2,1)S(1)}, u32[]{:S(2)}, u32[]{:S(2)}) async-start(bf16[16,8,4096]{2,1,0:T(8,128)(2,1)} %shard_map.94), calls=%async_computation | async-start | bytes 2097152 | tf_op jit(solution)/shard_map/all_to_all | solution.py:330
  19.9 1.9 %collective-permute-start.1 = (bf16[400,256]{1,0:T(8,128)(2,1)}, bf16[400,256]{1,0:T(8,128)(2,1)S(1)}, u32[]{:S(2)}, u32[]{:S(2)}) collective-permute-start(bf16[400,256]{1,0:T(8,128)(2,1)} %collective-permute-done), channel_id=1, source_target_pairs={{0,0},{1,257},{2,34},{3,291},{4,68},{5,325},{6,102},{7,359},{8,136... | collective-permute-start | bytes 614408 | tf_op jit(solution)/shard_map/ppermute | solution.py:308
  21.8 11.7 %all-to-all-done = bf16[16,8,4096]{2,1,0:T(8,128)(2,1)S(1)} async-done(((bf16[16,8,4096]{2,1,0:T(8,128)(2,1)}), bf16[16,8,4096]{2,1,0:T(8,128)(2,1)S(1)}, u32[]{:S(2)}, u32[]{:S(2)}) %all-to-all-start) | async-done | bytes 1048608 | tf_op jit(solution)/shard_map/all_to_all | solution.py:330
  33.5 0.0 copy-done
  33.5 0.8 convolution_convert_fusion.1
  34.3 0.1 collective-permute-done.1.qkv_ref
  34.4 1.0 shard_map.95
  35.4 11.3 %all-to-all-start.1 = ((bf16[32,112,128]{2,1,0:T(8,128)(2,1)}), bf16[32,112,128]{2,1,0:T(8,128)(2,1)S(1)}, u32[]{:S(2)}, u32[]{:S(2)}) async-start(bf16[32,112,128]{2,1,0:T(8,128)(2,1)} %shard_map.95), calls=%async_computation.1 | async-start | bytes 1835008 | tf_op jit(solution)/shard_map/all_to_all | solution.py:337
  46.8 9.6 %collective-permute-start.2 = (bf16[128,256]{1,0:T(8,128)(2,1)S(1)}, bf16[128,256]{1,0:T(8,128)(2,1)S(1)}, u32[]{:S(2)}, u32[]{:S(2)}) collective-permute-start(bf16[128,256]{1,0:T(8,128)(2,1)S(1)} %convolution_convert_fusion.1), channel_id=1, source_target_pairs={{0,0},{1,257},{2,34},{3,291},{4,68},{5,325},{6,102},{7,359},{8,136... | collective-permute-start | bytes 196616 | tf_op jit(solution)/shard_map/ppermute | solution.py:308
  56.4 0.1 pad_add_fusion.pos_ref
  56.5 6.9 %all-to-all-done.1.x_ref = bf16[32,112,128]{2,1,0:T(8,128)(2,1)S(1)} async-done(((bf16[32,112,128]{2,1,0:T(8,128)(2,1)}), bf16[32,112,128]{2,1,0:T(8,128)(2,1)S(1)}, u32[]{:S(2)}, u32[]{:S(2)}) %all-to-all-start.1) | async-done | bytes 917536 | tf_op jit(solution)/shard_map/all_to_all | solution.py:337
  63.3 4.1 %shard_map.96 = bf16[32,48,128]{2,1,0:T(8,128)(2,1)S(1)} custom-call(s32[4]{0:T(128)S(1)} %pad_add_fusion.pos_ref, bf16[32,112,128]{2,1,0:T(8,128)(2,1)S(1)} %all-to-all-done.1.x_ref), custom_call_target="tpu_custom_call" | custom-call | flops 536870912 | bytes 1310736 | tf_op jit(solution)/shard_map/pallas_call | solution.py:279
  67.4 0.0 collective-permute-done.2.da_ref
  67.4 14.3 %all_to_all.30.o_ref = bf16[32,48,128]{2,1,0:T(8,128)(2,1)S(1)} all-to-all(bf16[32,48,128]{2,1,0:T(8,128)(2,1)S(1)} %shard_map.96), channel_id=1, replica_groups=mesh['z'=16,'xh'=2,'y'=4,'xl'=2,'core'=2] {'xh','y','xl','core'}, dimensions={0} | all-to-all | bytes 786432 | tf_op jit(solution)/shard_map/all_to_all | solution.py:354
  81.8 0.4 shard_map.97
  82.2 14.1 %all_to_all.31.d_ref = bf16[32,48,128]{2,1,0:T(8,128)(2,1)S(1)} all-to-all(bf16[32,48,128]{2,1,0:T(8,128)(2,1)S(1)} %get-tuple-element.20), channel_id=1, replica_groups=mesh['z'=16,'xh'=2,'y'=4,'xl'=2,'core'=2] {'xh','y','xl','core'}, dimensions={0} | all-to-all | bytes 786432 | tf_op jit(solution)/shard_map/all_to_all | solution.py:360
  96.3 4.3 %shard_map.98 = bf16[32,96,128]{2,1,0:T(8,128)(2,1)S(1)} custom-call(s32[4]{0:T(128)S(1)} %pad_add_fusion.pos_ref, bf16[32,112,128]{2,1,0:T(8,128)(2,1)S(1)} %all-to-all-done.1.x_ref, bf16[32,48,128]{2,1,0:T(8,128)(2,1)S(1)} %all_to_all.31.d_ref), custom_call_target="tpu_custom_call" | custom-call | flops 1342177280 | bytes 2097168 | tf_op jit(solution)/shard_map/pallas_call | solution.py:279
  100.6 0.0 copy-start.1
  100.6 0.9 copy-done.1
  101.5 8.0 %all-to-all-start.4 = ((bf16[32,96,128]{2,1,0:T(8,128)(2,1)}), bf16[32,96,128]{2,1,0:T(8,128)(2,1)S(1)}, u32[]{:S(2)}, u32[]{:S(2)}) async-start(bf16[32,96,128]{2,1,0:T(8,128)(2,1)} %copy-done.1), calls=%async_computation.4 | async-start | bytes 1572864 | tf_op jit(solution)/shard_map/all_to_all | solution.py:365
  109.5 1.9 %collective-permute-start.3 = (bf16[128,256]{1,0:T(8,128)(2,1)S(1)}, bf16[128,256]{1,0:T(8,128)(2,1)S(1)}, u32[]{:S(2)}, u32[]{:S(2)}) collective-permute-start(bf16[128,256]{1,0:T(8,128)(2,1)S(1)} %get-tuple-element.21), channel_id=1, source_target_pairs={{0,0},{257,1},{34,2},{291,3},{68,4},{325,5},{102,6},{359,7},{136,8... | collective-permute-start | bytes 196616 | tf_op jit(solution)/shard_map/ppermute | solution.py:308
  111.4 15.8 %collective-permute-done.3 = bf16[128,256]{1,0:T(8,128)(2,1)S(1)} collective-permute-done((bf16[128,256]{1,0:T(8,128)(2,1)S(1)}, bf16[128,256]{1,0:T(8,128)(2,1)S(1)}, u32[]{:S(2)}, u32[]{:S(2)}) %collective-permute-start.3) | collective-permute-done | bytes 65568 | tf_op jit(solution)/shard_map/ppermute | solution.py:308
  127.2 0.0 all-to-all-done.4.grad_ref
  127.2 1.4 fusion
  128.7 5.5 %all-to-all-start.5 = ((bf16[16,8,4096]{2,1,0:T(8,128)(2,1)}), bf16[16,8,4096]{2,1,0:T(8,128)(2,1)}, u32[]{:S(2)}, u32[]{:S(2)}) async-start(bf16[16,8,4096]{2,1,0:T(8,128)(2,1)} %fusion), calls=%async_computation.5 | async-start | bytes 2097152 | tf_op jit(solution)/shard_map/all_to_all | solution.py:369
  134.1 0.1 shard_map.99
  134.3 1.9 %collective-permute-start.4 = (bf16[384,256]{1,0:T(8,128)(2,1)S(1)}, bf16[384,256]{1,0:T(8,128)(2,1)S(1)}, u32[]{:S(2)}, u32[]{:S(2)}) collective-permute-start(bf16[384,256]{1,0:T(8,128)(2,1)S(1)} %shard_map.99), channel_id=1, source_target_pairs={{0,0},{257,1},{34,2},{291,3},{68,4},{325,5},{102,6},{359,7},{136,8... | collective-permute-start | bytes 589832 | tf_op jit(solution)/shard_map/ppermute | solution.py:308
  136.2 20.3 %collective-permute-done.4 = bf16[384,256]{1,0:T(8,128)(2,1)S(1)} collective-permute-done((bf16[384,256]{1,0:T(8,128)(2,1)S(1)}, bf16[384,256]{1,0:T(8,128)(2,1)S(1)}, u32[]{:S(2)}, u32[]{:S(2)}) %collective-permute-start.4) | collective-permute-done | bytes 196640 | tf_op jit(solution)/shard_map/ppermute | solution.py:308
  156.4 0.7 fusion.2
  157.1 0.0 all-to-all-done.5
  157.1 2.0 %reduce_sum.12 = bf16[8,4096]{1,0:T(8,128)(2,1)} reduce(bf16[16,8,4096]{2,1,0:T(8,128)(2,1)} %all-to-all-done.5, bf16[]{:T(256)} %constant.20.clone.1), dimensions={0}, to_apply=%region_0.0 | reduce | flops 491520 | bytes 1114114 | tf_op jit(solution)/shard_map/reduce_sum | solution.py:370
Async XLA Ops:
  0.6 32.9 %copy-start = (bf16[256,4096]{1,0:T(8,128)(2,1)S(1)}, bf16[256,4096]{1,0:T(8,128)(2,1)}, u32[]{:S(2)}) copy-start(bf16[256,4096]{1,0:T(8,128)(2,1)} %param.10) | copy-start | bytes 6291460
  2.4 10.6 %collective-permute-start = (bf16[400,256]{1,0:T(8,128)(2,1)}, bf16[400,256]{1,0:T(8,128)(2,1)}, u32[]{:S(2)}, u32[]{:S(2)}) collective-permute-start(bf16[400,256]{1,0:T(8,128)(2,1)} %shard_map.93), channel_id=1, source_target_pairs={{0,0},{1,1},{2,2},{3,3},{4,4},{5,5},{6,6},{7,7},{8,8},{9,9},{10,10... | collective-permute-start | bytes 614408 | tf_op jit(solution)/shard_map/ppermute | solution.py:308
  13.0 20.5 %all-to-all-start = ((bf16[16,8,4096]{2,1,0:T(8,128)(2,1)}), bf16[16,8,4096]{2,1,0:T(8,128)(2,1)S(1)}, u32[]{:S(2)}, u32[]{:S(2)}) async-start(bf16[16,8,4096]{2,1,0:T(8,128)(2,1)} %shard_map.94), calls=%async_computation | async-start | bytes 2097152 | tf_op jit(solution)/shard_map/all_to_all | solution.py:330
  19.9 14.5 %collective-permute-start.1 = (bf16[400,256]{1,0:T(8,128)(2,1)}, bf16[400,256]{1,0:T(8,128)(2,1)S(1)}, u32[]{:S(2)}, u32[]{:S(2)}) collective-permute-start(bf16[400,256]{1,0:T(8,128)(2,1)} %collective-permute-done), channel_id=1, source_target_pairs={{0,0},{1,257},{2,34},{3,291},{4,68},{5,325},{6,102},{7,359},{8,136... | collective-permute-start | bytes 614408 | tf_op jit(solution)/shard_map/ppermute | solution.py:308
  35.4 27.9 %all-to-all-start.1 = ((bf16[32,112,128]{2,1,0:T(8,128)(2,1)}), bf16[32,112,128]{2,1,0:T(8,128)(2,1)S(1)}, u32[]{:S(2)}, u32[]{:S(2)}) async-start(bf16[32,112,128]{2,1,0:T(8,128)(2,1)} %shard_map.95), calls=%async_computation.1 | async-start | bytes 1835008 | tf_op jit(solution)/shard_map/all_to_all | solution.py:337
  46.8 20.6 %collective-permute-start.2 = (bf16[128,256]{1,0:T(8,128)(2,1)S(1)}, bf16[128,256]{1,0:T(8,128)(2,1)S(1)}, u32[]{:S(2)}, u32[]{:S(2)}) collective-permute-start(bf16[128,256]{1,0:T(8,128)(2,1)S(1)} %convolution_convert_fusion.1), channel_id=1, source_target_pairs={{0,0},{1,257},{2,34},{3,291},{4,68},{5,325},{6,102},{7,359},{8,136... | collective-permute-start | bytes 196616 | tf_op jit(solution)/shard_map/ppermute | solution.py:308
  100.6 0.9 copy-start.1
  101.5 25.7 %all-to-all-start.4 = ((bf16[32,96,128]{2,1,0:T(8,128)(2,1)}), bf16[32,96,128]{2,1,0:T(8,128)(2,1)S(1)}, u32[]{:S(2)}, u32[]{:S(2)}) async-start(bf16[32,96,128]{2,1,0:T(8,128)(2,1)} %copy-done.1), calls=%async_computation.4 | async-start | bytes 1572864 | tf_op jit(solution)/shard_map/all_to_all | solution.py:365
  109.5 17.7 %collective-permute-start.3 = (bf16[128,256]{1,0:T(8,128)(2,1)S(1)}, bf16[128,256]{1,0:T(8,128)(2,1)S(1)}, u32[]{:S(2)}, u32[]{:S(2)}) collective-permute-start(bf16[128,256]{1,0:T(8,128)(2,1)S(1)} %get-tuple-element.21), channel_id=1, source_target_pairs={{0,0},{257,1},{34,2},{291,3},{68,4},{325,5},{102,6},{359,7},{136,8... | collective-permute-start | bytes 196616 | tf_op jit(solution)/shard_map/ppermute | solution.py:308
  128.7 28.5 %all-to-all-start.5 = ((bf16[16,8,4096]{2,1,0:T(8,128)(2,1)}), bf16[16,8,4096]{2,1,0:T(8,128)(2,1)}, u32[]{:S(2)}, u32[]{:S(2)}) async-start(bf16[16,8,4096]{2,1,0:T(8,128)(2,1)} %fusion), calls=%async_computation.5 | async-start | bytes 2097152 | tf_op jit(solution)/shard_map/all_to_all | solution.py:369
  134.3 22.2 %collective-permute-start.4 = (bf16[384,256]{1,0:T(8,128)(2,1)S(1)}, bf16[384,256]{1,0:T(8,128)(2,1)S(1)}, u32[]{:S(2)}, u32[]{:S(2)}) collective-permute-start(bf16[384,256]{1,0:T(8,128)(2,1)S(1)} %shard_map.99), channel_id=1, source_target_pairs={{0,0},{257,1},{34,2},{291,3},{68,4},{325,5},{102,6},{359,7},{136,8... | collective-permute-start | bytes 589832 | tf_op jit(solution)/shard_map/ppermute | solution.py:308

commit v5 on v4

--- a/solution.py
+++ b/solution.py
@@ -362,8 +362,8 @@
         flops=10 * total * total * HD,
         smem=1,
     )
-    grad_parts, attn = lax.optimization_barrier((swap(grad_slots, PLANE), attn))
-    (grads,) = call(grads_kernel, [low(3 * rows, width)], (grad_parts,))
+    grad_slots, attn = lax.optimization_barrier((grad_slots, attn))
+    (grads,) = call(grads_kernel, [low(3 * rows, width)], (swap(grad_slots, PLANE),))
     grads = move(grads, back)
     partial = jnp.dot(attn, out_weight, preferred_element_type=f32).astype(bf16)
     parts = swap(partial.reshape((PLANES,) + d_out.shape), HEAD)

time: 160 us -> 161 us (level)
  the two profiles are of different devices: /device:TPU:183 before, /device:TPU:179 now
where the time goes in v5:
time: 161 us; the launch traced here: 160 us
  waiting for transfers between devices  67 us (42%)
  starting transfers between devices  57.3 us (36%)
  blocking collectives  14.5 us (9%)
  Pallas kernels  13.7 us (9%)
  local copies, waits for them, and re-layouts  2.36 us (1%)
  matrix products  2.27 us (1%)
  other arithmetic  2.09 us (1%)
    ppermute x5, waiting for transfers between devices, on_device(): move = lambda x, pairs: lax.ppermute(x, TURN, pairs)  32.5 us
    ppermute x5, starting transfers between devices, on_device(): move = lambda x, pairs: lax.ppermute(x, TURN, pairs)  17.1 us
    all_to_all x1, blocking collectives, on_device(): swap(o_slots, PLANE)  14.5 us
    pallas_call x7, Pallas kernels, call(): pl.pallas_call(kernel, out_shape=outs, in_specs=[SMEM] * smem + [space] *...  13.7 us
    all_to_all x1, waiting for transfers between devices, on_device(): d_out_all = swap(d_slots, HEAD)  11.7 us
    all_to_all x1, starting transfers between devices, on_device(): held = swap(slots, PLANE)  11.3 us
    all_to_all x1, waiting for transfers between devices, on_device(): swap(grad_slots, PLANE)  9.4 us
    all_to_all x1, starting transfers between devices, on_device(): parts = swap(partial.reshape((PLANES,) + d_out.shape), HEAD)  7.91 us
  transfers between devices with their start and end apart: 10, of which 8 were waited for; matrix products, arithmetic and copies ran while one was open for 2% of the time, Pallas kernels for 7%

profile of v5, /device:TPU:179, one launch (start us, length us, event | category | flops | bytes accessed | tf_op | source)
XLA Modules:
  0.0 160.0 jit_solution(11030609310375028891)
XLA Ops:
  0.6 0.0 copy-start
  0.6 1.8 %shard_map.93 = bf16[400,256]{1,0:T(8,128)(2,1)} custom-call(bf16[128,256]{1,0:T(8,128)(2,1)} %q_ref.1, bf16[128,256]{1,0:T(8,128)(2,1)} %k_ref.1, bf16[128,256]{1,0:T(8,128)(2,1)} %v_ref.1, s32[1,128]{1,0:T(1,128)} %bitcast.13), custom_call_target="tpu_custom_call" | custom-call | bytes 401920 | tf_op jit(solution)/shard_map/pallas_call | solution.py:279
  2.4 1.9 %collective-permute-start = (bf16[400,256]{1,0:T(8,128)(2,1)}, bf16[400,256]{1,0:T(8,128)(2,1)}, u32[]{:S(2)}, u32[]{:S(2)}) collective-permute-start(bf16[400,256]{1,0:T(8,128)(2,1)} %shard_map.93), channel_id=1, source_target_pairs={{0,0},{1,1},{2,2},{3,3},{4,4},{5,5},{6,6},{7,7},{8,8},{9,9},{10,10... | collective-permute-start | bytes 614408 | tf_op jit(solution)/shard_map/ppermute | solution.py:308
  4.4 1.9 %shard_map.94 = bf16[16,8,4096]{2,1,0:T(8,128)(2,1)} custom-call(bf16[8,4096]{1,0:T(8,128)(2,1)} %d_ref.1), custom_call_target="tpu_custom_call" | custom-call | bytes 1114112 | tf_op jit(solution)/shard_map/pallas_call | solution.py:279
  6.3 6.7 %collective-permute-done = bf16[400,256]{1,0:T(8,128)(2,1)} collective-permute-done((bf16[400,256]{1,0:T(8,128)(2,1)}, bf16[400,256]{1,0:T(8,128)(2,1)}, u32[]{:S(2)}, u32[]{:S(2)}) %collective-permute-start) | collective-permute-done | bytes 204832 | tf_op jit(solution)/shard_map/ppermute | solution.py:308
  13.0 6.9 %all-to-all-start = ((bf16[16,8,4096]{2,1,0:T(8,128)(2,1)}), bf16[16,8,4096]{2,1,0:T(8,128)(2,1)S(1)}, u32[]{:S(2)}, u32[]{:S(2)}) async-start(bf16[16,8,4096]{2,1,0:T(8,128)(2,1)} %shard_map.94), calls=%async_computation | async-start | bytes 2097152 | tf_op jit(solution)/shard_map/all_to_all | solution.py:330
  19.9 1.9 %collective-permute-start.1 = (bf16[400,256]{1,0:T(8,128)(2,1)}, bf16[400,256]{1,0:T(8,128)(2,1)S(1)}, u32[]{:S(2)}, u32[]{:S(2)}) collective-permute-start(bf16[400,256]{1,0:T(8,128)(2,1)} %collective-permute-done), channel_id=1, source_target_pairs={{0,0},{1,257},{2,34},{3,291},{4,68},{5,325},{6,102},{7,359},{8,136... | collective-permute-start | bytes 614408 | tf_op jit(solution)/shard_map/ppermute | solution.py:308
  21.8 11.7 %all-to-all-done = bf16[16,8,4096]{2,1,0:T(8,128)(2,1)S(1)} async-done(((bf16[16,8,4096]{2,1,0:T(8,128)(2,1)}), bf16[16,8,4096]{2,1,0:T(8,128)(2,1)S(1)}, u32[]{:S(2)}, u32[]{:S(2)}) %all-to-all-start) | async-done | bytes 1048608 | tf_op jit(solution)/shard_map/all_to_all | solution.py:330
  33.5 0.0 copy-done
  33.5 0.8 convolution_convert_fusion.1
  34.3 0.1 collective-permute-done.1.qkv_ref
  34.4 1.0 shard_map.95
  35.4 11.3 %all-to-all-start.1 = ((bf16[32,112,128]{2,1,0:T(8,128)(2,1)}), bf16[32,112,128]{2,1,0:T(8,128)(2,1)S(1)}, u32[]{:S(2)}, u32[]{:S(2)}) async-start(bf16[32,112,128]{2,1,0:T(8,128)(2,1)} %shard_map.95), calls=%async_computation.1 | async-start | bytes 1835008 | tf_op jit(solution)/shard_map/all_to_all | solution.py:337
  46.8 9.1 %collective-permute-start.2 = (bf16[128,256]{1,0:T(8,128)(2,1)S(1)}, bf16[128,256]{1,0:T(8,128)(2,1)S(1)}, u32[]{:S(2)}, u32[]{:S(2)}) collective-permute-start(bf16[128,256]{1,0:T(8,128)(2,1)S(1)} %convolution_convert_fusion.1), channel_id=1, source_target_pairs={{0,0},{1,257},{2,34},{3,291},{4,68},{5,325},{6,102},{7,359},{8,136... | collective-permute-start | bytes 196616 | tf_op jit(solution)/shard_map/ppermute | solution.py:308
  55.9 0.1 pad_add_fusion.pos_ref
  56.0 7.9 %all-to-all-done.1.x_ref = bf16[32,112,128]{2,1,0:T(8,128)(2,1)S(1)} async-done(((bf16[32,112,128]{2,1,0:T(8,128)(2,1)}), bf16[32,112,128]{2,1,0:T(8,128)(2,1)S(1)}, u32[]{:S(2)}, u32[]{:S(2)}) %all-to-all-start.1) | async-done | bytes 917536 | tf_op jit(solution)/shard_map/all_to_all | solution.py:337
  63.9 4.1 %shard_map.96 = bf16[32,48,128]{2,1,0:T(8,128)(2,1)S(1)} custom-call(s32[4]{0:T(128)S(1)} %pad_add_fusion.pos_ref, bf16[32,112,128]{2,1,0:T(8,128)(2,1)S(1)} %all-to-all-done.1.x_ref), custom_call_target="tpu_custom_call" | custom-call | flops 536870912 | bytes 1310736 | tf_op jit(solution)/shard_map/pallas_call | solution.py:279
  68.0 0.0 collective-permute-done.2.da_ref
  68.0 14.5 %all_to_all.30.o_ref = bf16[32,48,128]{2,1,0:T(8,128)(2,1)S(1)} all-to-all(bf16[32,48,128]{2,1,0:T(8,128)(2,1)S(1)} %shard_map.96), channel_id=1, replica_groups=mesh['z'=16,'xh'=2,'y'=4,'xl'=2,'core'=2] {'xh','y','xl','core'}, dimensions={0} | all-to-all | bytes 786432 | tf_op jit(solution)/shard_map/all_to_all | solution.py:354
  82.5 0.4 shard_map.97
  82.9 0.0 copy-start.2
  82.9 0.7 copy-done.2
  83.7 7.1 %all-to-all-start.3 = ((bf16[32,48,128]{2,1,0:T(8,128)(2,1)}), bf16[32,48,128]{2,1,0:T(8,128)(2,1)S(1)}, u32[]{:S(2)}, u32[]{:S(2)}) async-start(bf16[32,48,128]{2,1,0:T(8,128)(2,1)} %copy-done.2), calls=%async_computation.3 | async-start | bytes 786432 | tf_op jit(solution)/shard_map/all_to_all | solution.py:360
  90.8 1.9 %collective-permute-start.3 = (bf16[128,256]{1,0:T(8,128)(2,1)S(1)}, bf16[128,256]{1,0:T(8,128)(2,1)S(1)}, u32[]{:S(2)}, u32[]{:S(2)}) collective-permute-start(bf16[128,256]{1,0:T(8,128)(2,1)S(1)} %get-tuple-element.21), channel_id=1, source_target_pairs={{0,0},{257,1},{34,2},{291,3},{68,4},{325,5},{102,6},{359,7},{136,8... | collective-permute-start | bytes 196616 | tf_op jit(solution)/shard_map/ppermute | solution.py:308
  92.8 5.5 %all-to-all-done.3.d_ref = bf16[32,48,128]{2,1,0:T(8,128)(2,1)S(1)} async-done(((bf16[32,48,128]{2,1,0:T(8,128)(2,1)}), bf16[32,48,128]{2,1,0:T(8,128)(2,1)S(1)}, u32[]{:S(2)}, u32[]{:S(2)}) %all-to-all-start.3) | async-done | bytes 393248 | tf_op jit(solution)/shard_map/all_to_all | solution.py:360
  98.2 4.4 %shard_map.98 = bf16[32,96,128]{2,1,0:T(8,128)(2,1)S(1)} custom-call(s32[4]{0:T(128)S(1)} %pad_add_fusion.pos_ref, bf16[32,112,128]{2,1,0:T(8,128)(2,1)S(1)} %all-to-all-done.1.x_ref, bf16[32,48,128]{2,1,0:T(8,128)(2,1)S(1)} %all-to-all-done.3.d_ref), custom_call_target="tpu_custom_call" | custom-call | flops 1342177280 | bytes 2097168 | tf_op jit(solution)/shard_map/pallas_call | solution.py:279
  102.6 0.0 copy-start.1
  102.6 0.9 copy-done.1
  103.5 5.0 %collective-permute-done.3 = bf16[128,256]{1,0:T(8,128)(2,1)S(1)} collective-permute-done((bf16[128,256]{1,0:T(8,128)(2,1)S(1)}, bf16[128,256]{1,0:T(8,128)(2,1)S(1)}, u32[]{:S(2)}, u32[]{:S(2)}) %collective-permute-start.3) | collective-permute-done | bytes 65568 | tf_op jit(solution)/shard_map/ppermute | solution.py:308
  108.6 6.9 %all-to-all-start.5 = ((bf16[32,96,128]{2,1,0:T(8,128)(2,1)}), bf16[32,96,128]{2,1,0:T(8,128)(2,1)S(1)}, u32[]{:S(2)}, u32[]{:S(2)}) async-start(bf16[32,96,128]{2,1,0:T(8,128)(2,1)} %copy-done.1), calls=%async_computation.5 | async-start | bytes 1572864 | tf_op jit(solution)/shard_map/all_to_all | solution.py:366
  115.5 1.4 fusion
  116.9 9.4 %all-to-all-done.5.grad_ref = bf16[32,96,128]{2,1,0:T(8,128)(2,1)S(1)} async-done(((bf16[32,96,128]{2,1,0:T(8,128)(2,1)}), bf16[32,96,128]{2,1,0:T(8,128)(2,1)S(1)}, u32[]{:S(2)}, u32[]{:S(2)}) %all-to-all-start.5) | async-done | bytes 786464 | tf_op jit(solution)/shard_map/all_to_all | solution.py:366
  126.3 7.9 %all-to-all-start.4 = ((bf16[16,8,4096]{2,1,0:T(8,128)(2,1)}), bf16[16,8,4096]{2,1,0:T(8,128)(2,1)}, u32[]{:S(2)}, u32[]{:S(2)}) async-start(bf16[16,8,4096]{2,1,0:T(8,128)(2,1)} %fusion), calls=%async_computation.4 | async-start | bytes 2097152 | tf_op jit(solution)/shard_map/all_to_all | solution.py:369
  134.3 0.1 shard_map.99
  134.4 2.2 %collective-permute-start.4 = (bf16[384,256]{1,0:T(8,128)(2,1)S(1)}, bf16[384,256]{1,0:T(8,128)(2,1)S(1)}, u32[]{:S(2)}, u32[]{:S(2)}) collective-permute-start(bf16[384,256]{1,0:T(8,128)(2,1)S(1)} %shard_map.99), channel_id=1, source_target_pairs={{0,0},{257,1},{34,2},{291,3},{68,4},{325,5},{102,6},{359,7},{136,8... | collective-permute-start | bytes 589832 | tf_op jit(solution)/shard_map/ppermute | solution.py:308
  136.6 20.7 %collective-permute-done.4 = bf16[384,256]{1,0:T(8,128)(2,1)S(1)} collective-permute-done((bf16[384,256]{1,0:T(8,128)(2,1)S(1)}, bf16[384,256]{1,0:T(8,128)(2,1)S(1)}, u32[]{:S(2)}, u32[]{:S(2)}) %collective-permute-start.4) | collective-permute-done | bytes 196640 | tf_op jit(solution)/shard_map/ppermute | solution.py:308
  157.3 0.7 fusion.2
  158.0 0.0 all-to-all-done.4
  158.0 2.0 %reduce_sum.12 = bf16[8,4096]{1,0:T(8,128)(2,1)} reduce(bf16[16,8,4096]{2,1,0:T(8,128)(2,1)} %all-to-all-done.4, bf16[]{:T(256)} %constant.20.clone.1), dimensions={0}, to_apply=%region_0.0 | reduce | flops 491520 | bytes 1114114 | tf_op jit(solution)/shard_map/reduce_sum | solution.py:370
Async XLA Ops:
  0.6 32.9 %copy-start = (bf16[256,4096]{1,0:T(8,128)(2,1)S(1)}, bf16[256,4096]{1,0:T(8,128)(2,1)}, u32[]{:S(2)}) copy-start(bf16[256,4096]{1,0:T(8,128)(2,1)} %param.10) | copy-start | bytes 6291460
  2.4 10.6 %collective-permute-start = (bf16[400,256]{1,0:T(8,128)(2,1)}, bf16[400,256]{1,0:T(8,128)(2,1)}, u32[]{:S(2)}, u32[]{:S(2)}) collective-permute-start(bf16[400,256]{1,0:T(8,128)(2,1)} %shard_map.93), channel_id=1, source_target_pairs={{0,0},{1,1},{2,2},{3,3},{4,4},{5,5},{6,6},{7,7},{8,8},{9,9},{10,10... | collective-permute-start | bytes 614408 | tf_op jit(solution)/shard_map/ppermute | solution.py:308
  13.0 20.5 %all-to-all-start = ((bf16[16,8,4096]{2,1,0:T(8,128)(2,1)}), bf16[16,8,4096]{2,1,0:T(8,128)(2,1)S(1)}, u32[]{:S(2)}, u32[]{:S(2)}) async-start(bf16[16,8,4096]{2,1,0:T(8,128)(2,1)} %shard_map.94), calls=%async_computation | async-start | bytes 2097152 | tf_op jit(solution)/shard_map/all_to_all | solution.py:330
  19.9 14.5 %collective-permute-start.1 = (bf16[400,256]{1,0:T(8,128)(2,1)}, bf16[400,256]{1,0:T(8,128)(2,1)S(1)}, u32[]{:S(2)}, u32[]{:S(2)}) collective-permute-start(bf16[400,256]{1,0:T(8,128)(2,1)} %collective-permute-done), channel_id=1, source_target_pairs={{0,0},{1,257},{2,34},{3,291},{4,68},{5,325},{6,102},{7,359},{8,136... | collective-permute-start | bytes 614408 | tf_op jit(solution)/shard_map/ppermute | solution.py:308
  35.4 28.5 %all-to-all-start.1 = ((bf16[32,112,128]{2,1,0:T(8,128)(2,1)}), bf16[32,112,128]{2,1,0:T(8,128)(2,1)S(1)}, u32[]{:S(2)}, u32[]{:S(2)}) async-start(bf16[32,112,128]{2,1,0:T(8,128)(2,1)} %shard_map.95), calls=%async_computation.1 | async-start | bytes 1835008 | tf_op jit(solution)/shard_map/all_to_all | solution.py:337
  46.8 21.2 %collective-permute-start.2 = (bf16[128,256]{1,0:T(8,128)(2,1)S(1)}, bf16[128,256]{1,0:T(8,128)(2,1)S(1)}, u32[]{:S(2)}, u32[]{:S(2)}) collective-permute-start(bf16[128,256]{1,0:T(8,128)(2,1)S(1)} %convolution_convert_fusion.1), channel_id=1, source_target_pairs={{0,0},{1,257},{2,34},{3,291},{4,68},{5,325},{6,102},{7,359},{8,136... | collective-permute-start | bytes 196616 | tf_op jit(solution)/shard_map/ppermute | solution.py:308
  82.9 0.8 copy-start.2
  83.7 14.5 %all-to-all-start.3 = ((bf16[32,48,128]{2,1,0:T(8,128)(2,1)}), bf16[32,48,128]{2,1,0:T(8,128)(2,1)S(1)}, u32[]{:S(2)}, u32[]{:S(2)}) async-start(bf16[32,48,128]{2,1,0:T(8,128)(2,1)} %copy-done.2), calls=%async_computation.3 | async-start | bytes 786432 | tf_op jit(solution)/shard_map/all_to_all | solution.py:360
  90.8 17.7 %collective-permute-start.3 = (bf16[128,256]{1,0:T(8,128)(2,1)S(1)}, bf16[128,256]{1,0:T(8,128)(2,1)S(1)}, u32[]{:S(2)}, u32[]{:S(2)}) collective-permute-start(bf16[128,256]{1,0:T(8,128)(2,1)S(1)} %get-tuple-element.21), channel_id=1, source_target_pairs={{0,0},{257,1},{34,2},{291,3},{68,4},{325,5},{102,6},{359,7},{136,8... | collective-permute-start | bytes 196616 | tf_op jit(solution)/shard_map/ppermute | solution.py:308
  102.6 0.9 copy-start.1
  108.6 17.8 %all-to-all-start.5 = ((bf16[32,96,128]{2,1,0:T(8,128)(2,1)}), bf16[32,96,128]{2,1,0:T(8,128)(2,1)S(1)}, u32[]{:S(2)}, u32[]{:S(2)}) async-start(bf16[32,96,128]{2,1,0:T(8,128)(2,1)} %copy-done.1), calls=%async_computation.5 | async-start | bytes 1572864 | tf_op jit(solution)/shard_map/all_to_all | solution.py:366
  126.3 31.6 %all-to-all-start.4 = ((bf16[16,8,4096]{2,1,0:T(8,128)(2,1)}), bf16[16,8,4096]{2,1,0:T(8,128)(2,1)}, u32[]{:S(2)}, u32[]{:S(2)}) async-start(bf16[16,8,4096]{2,1,0:T(8,128)(2,1)} %fusion), calls=%async_computation.4 | async-start | bytes 2097152 | tf_op jit(solution)/shard_map/all_to_all | solution.py:369
  134.4 22.9 %collective-permute-start.4 = (bf16[384,256]{1,0:T(8,128)(2,1)S(1)}, bf16[384,256]{1,0:T(8,128)(2,1)S(1)}, u32[]{:S(2)}, u32[]{:S(2)}) collective-permute-start(bf16[384,256]{1,0:T(8,128)(2,1)S(1)} %shard_map.99), channel_id=1, source_target_pairs={{0,0},{257,1},{34,2},{291,3},{68,4},{325,5},{102,6},{359,7},{136,8... | collective-permute-start | bytes 589832 | tf_op jit(solution)/shard_map/ppermute | solution.py:308

commit v6 on v4

--- a/solution.py
+++ b/solution.py
@@ -267,6 +267,15 @@
             out_ref[rows, cols] = both[PIECE:].astype(bf16)
 
 
+def mixed_kernel(x_ref, out_ref, buf, sem):
+    copy = pltpu.make_async_copy(x_ref, buf, sem)
+    copy.start()
+    copy.wait()
+    for c in range(0, buf.shape[1], 512):
+        parts = buf[:, c : c + 512].astype(f32).reshape(PLANES, 8, 512)
+        out_ref[:, c : c + 512] = jnp.sum(parts, axis=0).astype(bf16)
+
+
 VMEM = pl.BlockSpec(memory_space=pltpu.VMEM)
 SMEM = pl.BlockSpec(memory_space=pltpu.SMEM)
 
@@ -331,7 +340,6 @@
     d_attn = lax.dot_general(
         d_out_all.reshape(rows, -1), out_weight, NT, preferred_element_type=f32
     ).astype(bf16)
-    qkv, d_attn = lax.optimization_barrier((qkv, d_attn))
     d_attn = move(d_attn, there)
     (slots,) = call(pack_kernel, [low(SHARES, 3 * PIECE + STAT, HD)], (qkv,))
     held = swap(slots, PLANE)
@@ -367,7 +375,14 @@
     grads = move(grads, back)
     partial = jnp.dot(attn, out_weight, preferred_element_type=f32).astype(bf16)
     parts = swap(partial.reshape((PLANES,) + d_out.shape), HEAD)
-    mixed = jnp.sum(parts.astype(f32), axis=0).astype(bf16)
+    (mixed,) = call(
+        mixed_kernel,
+        [low(*d_out.shape)],
+        (parts.reshape(rows, -1),),
+        [pltpu.VMEM((rows, d_out.shape[1]), bf16), pltpu.SemaphoreType.DMA],
+        space=HBM,
+        limit=60,
+    )
     return mixed, grads[:rows], grads[rows : 2 * rows], grads[2 * rows :]
 
 

time: 160 us -> 160 us (level)
  waiting for transfers between devices: 61.1 us -> 59 us
  Pallas kernels: 13.6 us -> 15.7 us
  other arithmetic: 2.09 us -> 0.08 us
    ppermute x5, waiting for transfers between devices: 42.6 us -> 55.1 us  [on_device(): move = lambda x, pairs: lax.ppermute(x, TURN, pairs)]
    all_to_all x1, waiting for transfers between devices: 11.7 us -> 0.01 us  [on_device(): d_out_all = swap(d_slots, HEAD)]
    all_to_all x1, waiting for transfers between devices: 6.87 us -> 3.96 us  [on_device(): held = swap(slots, PLANE)]
    pallas_call x7 -> x8, Pallas kernels: 13.6 us -> 15.7 us  [call(): pl.pallas_call(kernel, out_shape=outs, in_specs=[SMEM] * smem + [space] *...]
    reduce_sum x1 -> x0, other arithmetic: 2.01 us -> none  [on_device(): mixed = jnp.sum(parts.astype(f32), axis=0).astype(bf16)]
  transfers between devices with their start and end apart: 9 -> 9, of which waited for: 6 -> 5; matrix products, arithmetic and copies ran while one was open for 1% -> 2% of each run, Pallas kernels for 4% -> 4%
where the time goes in v6:
time: 160 us; the launch traced here: 159 us
  waiting for transfers between devices  59 us (37%)
  starting transfers between devices  49.2 us (31%)
  blocking collectives  28.4 us (18%)
  Pallas kernels  15.7 us (10%)
  matrix products  3.51 us (2%)
  local copies, waits for them, and re-layouts  2.56 us (2%)
    ppermute x5, waiting for transfers between devices, on_device(): move = lambda x, pairs: lax.ppermute(x, TURN, pairs)  55.1 us
    ppermute x5, starting transfers between devices, on_device(): move = lambda x, pairs: lax.ppermute(x, TURN, pairs)  17.6 us
    pallas_call x8, Pallas kernels, call(): pl.pallas_call(kernel, out_shape=outs, in_specs=[SMEM] * smem + [space] *...  15.7 us
    all_to_all x1, blocking collectives, on_device(): swap(o_slots, PLANE)  14.3 us
    all_to_all x1, blocking collectives, on_device(): swap(da_slots, PLANE)  14.1 us
    all_to_all x1, starting transfers between devices, on_device(): held = swap(slots, PLANE)  11.3 us
    all_to_all x1, starting transfers between devices, on_device(): grad_parts, attn = lax.optimization_barrier((swap(grad_slots, PLANE), attn))  7.96 us
    all_to_all x1, starting transfers between devices, on_device(): d_out_all = swap(d_slots, HEAD)  6.91 us
  transfers between devices with their start and end apart: 9, of which 5 were waited for; matrix products, arithmetic and copies ran while one was open for 2% of the time, Pallas kernels for 4%

profile of v6, /device:TPU:183, one launch (start us, length us, event | category | flops | bytes accessed | tf_op | source)
XLA Modules:
  0.0 159.3 jit_solution(11110982950661442797)
XLA Ops:
  0.6 0.0 copy-start
  0.6 1.8 %shard_map.93 = bf16[400,256]{1,0:T(8,128)(2,1)} custom-call(bf16[128,256]{1,0:T(8,128)(2,1)} %q_ref.1, bf16[128,256]{1,0:T(8,128)(2,1)} %k_ref.1, bf16[128,256]{1,0:T(8,128)(2,1)} %v_ref.1, s32[1,128]{1,0:T(1,128)} %bitcast.14), custom_call_target="tpu_custom_call" | custom-call | bytes 401920 | tf_op jit(solution)/shard_map/pallas_call | solution.py:288
  2.4 2.2 %collective-permute-start = (bf16[400,256]{1,0:T(8,128)(2,1)}, bf16[400,256]{1,0:T(8,128)(2,1)S(1)}, u32[]{:S(2)}, u32[]{:S(2)}) collective-permute-start(bf16[400,256]{1,0:T(8,128)(2,1)} %shard_map.93), channel_id=1, source_target_pairs={{0,0},{1,1},{2,2},{3,3},{4,4},{5,5},{6,6},{7,7},{8,8},{9,9},{10,10... | collective-permute-start | bytes 614408 | tf_op jit(solution)/shard_map/ppermute | solution.py:317
  4.7 1.9 %shard_map.94 = bf16[16,8,4096]{2,1,0:T(8,128)(2,1)} custom-call(bf16[8,4096]{1,0:T(8,128)(2,1)} %d_ref.1), custom_call_target="tpu_custom_call" | custom-call | bytes 1114112 | tf_op jit(solution)/shard_map/pallas_call | solution.py:288
  6.6 6.3 %collective-permute-done = bf16[400,256]{1,0:T(8,128)(2,1)S(1)} collective-permute-done((bf16[400,256]{1,0:T(8,128)(2,1)}, bf16[400,256]{1,0:T(8,128)(2,1)S(1)}, u32[]{:S(2)}, u32[]{:S(2)}) %collective-permute-start) | collective-permute-done | bytes 204832 | tf_op jit(solution)/shard_map/ppermute | solution.py:317
  12.9 6.9 %all-to-all-start.1 = ((bf16[16,8,4096]{2,1,0:T(8,128)(2,1)}), bf16[16,8,4096]{2,1,0:T(8,128)(2,1)S(1)}, u32[]{:S(2)}, u32[]{:S(2)}) async-start(bf16[16,8,4096]{2,1,0:T(8,128)(2,1)} %shard_map.94), calls=%async_computation.1 | async-start | bytes 2097152 | tf_op jit(solution)/shard_map/all_to_all | solution.py:339
  19.8 1.9 %collective-permute-start.1 = (bf16[400,256]{1,0:T(8,128)(2,1)S(1)}, bf16[400,256]{1,0:T(8,128)(2,1)S(1)}, u32[]{:S(2)}, u32[]{:S(2)}) collective-permute-start(bf16[400,256]{1,0:T(8,128)(2,1)S(1)} %collective-permute-done), channel_id=1, source_target_pairs={{0,0},{1,257},{2,34},{3,291},{4,68},{5,325},{6,102},{7,359},{8,136... | collective-permute-start | bytes 614408 | tf_op jit(solution)/shard_map/ppermute | solution.py:317
  21.7 12.4 %collective-permute-done.1.qkv_ref = bf16[400,256]{1,0:T(8,128)(2,1)S(1)} collective-permute-done((bf16[400,256]{1,0:T(8,128)(2,1)S(1)}, bf16[400,256]{1,0:T(8,128)(2,1)S(1)}, u32[]{:S(2)}, u32[]{:S(2)}) %collective-permute-start.1) | collective-permute-done | bytes 204832 | tf_op jit(solution)/shard_map/ppermute | solution.py:317
  34.1 1.1 shard_map.95
  35.2 0.0 all-to-all-done.1
  35.2 0.0 copy-start.2
  35.2 1.0 copy-done.2
  36.2 11.3 %all-to-all-start = ((bf16[32,112,128]{2,1,0:T(8,128)(2,1)}), bf16[32,112,128]{2,1,0:T(8,128)(2,1)S(1)}, u32[]{:S(2)}, u32[]{:S(2)}) async-start(bf16[32,112,128]{2,1,0:T(8,128)(2,1)} %shard_map.95), calls=%async_computation | async-start | bytes 1835008 | tf_op jit(solution)/shard_map/all_to_all | solution.py:345
  47.5 0.0 copy-done
  47.5 2.1 %convolution_convert_fusion.1 = bf16[128,256]{1,0:T(8,128)(2,1)S(1)} fusion(bf16[256,4096]{1,0:T(8,128)(2,1)S(1)} %copy-done, bf16[16,8,4096]{2,1,0:T(8,128)(2,1)} %copy-done.2), kind=kOutput, calls=%fused_computation.2 | convolution fusion | flops 268468224 | bytes 3211264 | tf_op jit(solution)/shard_map/dot_general | solution.py:340
  49.6 9.6 %collective-permute-start.2 = (bf16[128,256]{1,0:T(8,128)(2,1)S(1)}, bf16[128,256]{1,0:T(8,128)(2,1)S(1)}, u32[]{:S(2)}, u32[]{:S(2)}) collective-permute-start(bf16[128,256]{1,0:T(8,128)(2,1)S(1)} %convolution_convert_fusion.1), channel_id=1, source_target_pairs={{0,0},{1,257},{2,34},{3,291},{4,68},{5,325},{6,102},{7,359},{8,136... | collective-permute-start | bytes 196616 | tf_op jit(solution)/shard_map/ppermute | solution.py:317
  59.2 0.1 pad_add_fusion.pos_ref
  59.3 4.0 %all-to-all-done.x_ref = bf16[32,112,128]{2,1,0:T(8,128)(2,1)S(1)} async-done(((bf16[32,112,128]{2,1,0:T(8,128)(2,1)}), bf16[32,112,128]{2,1,0:T(8,128)(2,1)S(1)}, u32[]{:S(2)}, u32[]{:S(2)}) %all-to-all-start) | async-done | bytes 917536 | tf_op jit(solution)/shard_map/all_to_all | solution.py:345
  63.2 4.1 %shard_map.96 = bf16[32,48,128]{2,1,0:T(8,128)(2,1)S(1)} custom-call(s32[4]{0:T(128)S(1)} %pad_add_fusion.pos_ref, bf16[32,112,128]{2,1,0:T(8,128)(2,1)S(1)} %all-to-all-done.x_ref), custom_call_target="tpu_custom_call" | custom-call | flops 536870912 | bytes 1310736 | tf_op jit(solution)/shard_map/pallas_call | solution.py:288
  67.3 0.0 collective-permute-done.2.da_ref
  67.3 14.3 %all_to_all.30.o_ref = bf16[32,48,128]{2,1,0:T(8,128)(2,1)S(1)} all-to-all(bf16[32,48,128]{2,1,0:T(8,128)(2,1)S(1)} %shard_map.96), channel_id=1, replica_groups=mesh['z'=16,'xh'=2,'y'=4,'xl'=2,'core'=2] {'xh','y','xl','core'}, dimensions={0} | all-to-all | bytes 786432 | tf_op jit(solution)/shard_map/all_to_all | solution.py:362
  81.7 0.4 shard_map.97
  82.1 14.1 %all_to_all.31.d_ref = bf16[32,48,128]{2,1,0:T(8,128)(2,1)S(1)} all-to-all(bf16[32,48,128]{2,1,0:T(8,128)(2,1)S(1)} %get-tuple-element.16), channel_id=1, replica_groups=mesh['z'=16,'xh'=2,'y'=4,'xl'=2,'core'=2] {'xh','y','xl','core'}, dimensions={0} | all-to-all | bytes 786432 | tf_op jit(solution)/shard_map/all_to_all | solution.py:368
  96.1 4.3 %shard_map.98 = bf16[32,96,128]{2,1,0:T(8,128)(2,1)S(1)} custom-call(s32[4]{0:T(128)S(1)} %pad_add_fusion.pos_ref, bf16[32,112,128]{2,1,0:T(8,128)(2,1)S(1)} %all-to-all-done.x_ref, bf16[32,48,128]{2,1,0:T(8,128)(2,1)S(1)} %all_to_all.31.d_ref), custom_call_target="tpu_custom_call" | custom-call | flops 1342177280 | bytes 2097168 | tf_op jit(solution)/shard_map/pallas_call | solution.py:288
  100.5 0.0 copy-start.1
  100.5 0.9 copy-done.1
  101.4 8.0 %all-to-all-start.4 = ((bf16[32,96,128]{2,1,0:T(8,128)(2,1)}), bf16[32,96,128]{2,1,0:T(8,128)(2,1)S(1)}, u32[]{:S(2)}, u32[]{:S(2)}) async-start(bf16[32,96,128]{2,1,0:T(8,128)(2,1)} %copy-done.1), calls=%async_computation.4 | async-start | bytes 1572864 | tf_op jit(solution)/shard_map/all_to_all | solution.py:373
  109.4 1.9 %collective-permute-start.3 = (bf16[128,256]{1,0:T(8,128)(2,1)S(1)}, bf16[128,256]{1,0:T(8,128)(2,1)S(1)}, u32[]{:S(2)}, u32[]{:S(2)}) collective-permute-start(bf16[128,256]{1,0:T(8,128)(2,1)S(1)} %get-tuple-element.17), channel_id=1, source_target_pairs={{0,0},{257,1},{34,2},{291,3},{68,4},{325,5},{102,6},{359,7},{136,8... | collective-permute-start | bytes 196616 | tf_op jit(solution)/shard_map/ppermute | solution.py:317
  111.3 16.5 %collective-permute-done.3 = bf16[128,256]{1,0:T(8,128)(2,1)S(1)} collective-permute-done((bf16[128,256]{1,0:T(8,128)(2,1)S(1)}, bf16[128,256]{1,0:T(8,128)(2,1)S(1)}, u32[]{:S(2)}, u32[]{:S(2)}) %collective-permute-start.3) | collective-permute-done | bytes 65568 | tf_op jit(solution)/shard_map/ppermute | solution.py:317
  127.8 0.0 all-to-all-done.4.grad_ref
  127.8 1.5 fusion
  129.3 5.5 %all-to-all-start.5 = ((bf16[16,8,4096]{2,1,0:T(8,128)(2,1)}), bf16[16,8,4096]{2,1,0:T(8,128)(2,1)}, u32[]{:S(2)}, u32[]{:S(2)}) async-start(bf16[16,8,4096]{2,1,0:T(8,128)(2,1)} %fusion), calls=%async_computation.5 | async-start | bytes 2097152 | tf_op jit(solution)/shard_map/all_to_all | solution.py:377
  134.7 0.1 shard_map.100
  134.8 1.9 %collective-permute-start.4 = (bf16[384,256]{1,0:T(8,128)(2,1)S(1)}, bf16[384,256]{1,0:T(8,128)(2,1)S(1)}, u32[]{:S(2)}, u32[]{:S(2)}) collective-permute-start(bf16[384,256]{1,0:T(8,128)(2,1)S(1)} %shard_map.100), channel_id=1, source_target_pairs={{0,0},{257,1},{34,2},{291,3},{68,4},{325,5},{102,6},{359,7},{136,8... | collective-permute-start | bytes 589832 | tf_op jit(solution)/shard_map/ppermute | solution.py:317
  136.8 19.9 %collective-permute-done.4 = bf16[384,256]{1,0:T(8,128)(2,1)S(1)} collective-permute-done((bf16[384,256]{1,0:T(8,128)(2,1)S(1)}, bf16[384,256]{1,0:T(8,128)(2,1)S(1)}, u32[]{:S(2)}, u32[]{:S(2)}) %collective-permute-start.4) | collective-permute-done | bytes 196640 | tf_op jit(solution)/shard_map/ppermute | solution.py:317
  156.6 0.7 fusion.2
  157.3 0.0 all-to-all-done.5
  157.3 2.0 %shard_map.99 = bf16[8,4096]{1,0:T(8,128)(2,1)} custom-call(bf16[128,4096]{1,0:T(8,128)(2,1)} %bitcast.7.x_ref), custom_call_target="tpu_custom_call" | custom-call | bytes 1114112 | tf_op jit(solution)/shard_map/pallas_call | solution.py:288
Async XLA Ops:
  0.6 46.9 %copy-start = (bf16[256,4096]{1,0:T(8,128)(2,1)S(1)}, bf16[256,4096]{1,0:T(8,128)(2,1)}, u32[]{:S(2)}) copy-start(bf16[256,4096]{1,0:T(8,128)(2,1)} %param.10) | copy-start | bytes 6291460
  2.4 10.5 %collective-permute-start = (bf16[400,256]{1,0:T(8,128)(2,1)}, bf16[400,256]{1,0:T(8,128)(2,1)S(1)}, u32[]{:S(2)}, u32[]{:S(2)}) collective-permute-start(bf16[400,256]{1,0:T(8,128)(2,1)} %shard_map.93), channel_id=1, source_target_pairs={{0,0},{1,1},{2,2},{3,3},{4,4},{5,5},{6,6},{7,7},{8,8},{9,9},{10,10... | collective-permute-start | bytes 614408 | tf_op jit(solution)/shard_map/ppermute | solution.py:317
  12.9 22.3 %all-to-all-start.1 = ((bf16[16,8,4096]{2,1,0:T(8,128)(2,1)}), bf16[16,8,4096]{2,1,0:T(8,128)(2,1)S(1)}, u32[]{:S(2)}, u32[]{:S(2)}) async-start(bf16[16,8,4096]{2,1,0:T(8,128)(2,1)} %shard_map.94), calls=%async_computation.1 | async-start | bytes 2097152 | tf_op jit(solution)/shard_map/all_to_all | solution.py:339
  19.8 14.3 %collective-permute-start.1 = (bf16[400,256]{1,0:T(8,128)(2,1)S(1)}, bf16[400,256]{1,0:T(8,128)(2,1)S(1)}, u32[]{:S(2)}, u32[]{:S(2)}) collective-permute-start(bf16[400,256]{1,0:T(8,128)(2,1)S(1)} %collective-permute-done), channel_id=1, source_target_pairs={{0,0},{1,257},{2,34},{3,291},{4,68},{5,325},{6,102},{7,359},{8,136... | collective-permute-start | bytes 614408 | tf_op jit(solution)/shard_map/ppermute | solution.py:317
  35.2 1.0 copy-start.2
  36.2 27.1 %all-to-all-start = ((bf16[32,112,128]{2,1,0:T(8,128)(2,1)}), bf16[32,112,128]{2,1,0:T(8,128)(2,1)S(1)}, u32[]{:S(2)}, u32[]{:S(2)}) async-start(bf16[32,112,128]{2,1,0:T(8,128)(2,1)} %shard_map.95), calls=%async_computation | async-start | bytes 1835008 | tf_op jit(solution)/shard_map/all_to_all | solution.py:345
  49.6 17.7 %collective-permute-start.2 = (bf16[128,256]{1,0:T(8,128)(2,1)S(1)}, bf16[128,256]{1,0:T(8,128)(2,1)S(1)}, u32[]{:S(2)}, u32[]{:S(2)}) collective-permute-start(bf16[128,256]{1,0:T(8,128)(2,1)S(1)} %convolution_convert_fusion.1), channel_id=1, source_target_pairs={{0,0},{1,257},{2,34},{3,291},{4,68},{5,325},{6,102},{7,359},{8,136... | collective-permute-start | bytes 196616 | tf_op jit(solution)/shard_map/ppermute | solution.py:317
  100.5 0.9 copy-start.1
  101.4 26.4 %all-to-all-start.4 = ((bf16[32,96,128]{2,1,0:T(8,128)(2,1)}), bf16[32,96,128]{2,1,0:T(8,128)(2,1)S(1)}, u32[]{:S(2)}, u32[]{:S(2)}) async-start(bf16[32,96,128]{2,1,0:T(8,128)(2,1)} %copy-done.1), calls=%async_computation.4 | async-start | bytes 1572864 | tf_op jit(solution)/shard_map/all_to_all | solution.py:373
  109.4 18.4 %collective-permute-start.3 = (bf16[128,256]{1,0:T(8,128)(2,1)S(1)}, bf16[128,256]{1,0:T(8,128)(2,1)S(1)}, u32[]{:S(2)}, u32[]{:S(2)}) collective-permute-start(bf16[128,256]{1,0:T(8,128)(2,1)S(1)} %get-tuple-element.17), channel_id=1, source_target_pairs={{0,0},{257,1},{34,2},{291,3},{68,4},{325,5},{102,6},{359,7},{136,8... | collective-permute-start | bytes 196616 | tf_op jit(solution)/shard_map/ppermute | solution.py:317
  129.3 28.1 %all-to-all-start.5 = ((bf16[16,8,4096]{2,1,0:T(8,128)(2,1)}), bf16[16,8,4096]{2,1,0:T(8,128)(2,1)}, u32[]{:S(2)}, u32[]{:S(2)}) async-start(bf16[16,8,4096]{2,1,0:T(8,128)(2,1)} %fusion), calls=%async_computation.5 | async-start | bytes 2097152 | tf_op jit(solution)/shard_map/all_to_all | solution.py:377
  134.8 21.8 %collective-permute-start.4 = (bf16[384,256]{1,0:T(8,128)(2,1)S(1)}, bf16[384,256]{1,0:T(8,128)(2,1)S(1)}, u32[]{:S(2)}, u32[]{:S(2)}) collective-permute-start(bf16[384,256]{1,0:T(8,128)(2,1)S(1)} %shard_map.100), channel_id=1, source_target_pairs={{0,0},{257,1},{34,2},{291,3},{68,4},{325,5},{102,6},{359,7},{136,8... | collective-permute-start | bytes 589832 | tf_op jit(solution)/shard_map/ppermute | solution.py:317
